TPU v7x, 256 devices: a whole 4x4x8 slice. The times are simulated.
256 devices in a mesh: region: 8 (over x, core), sub: 32 (over y, z).
Axes of the slice: x: 4, y: 4, z: 8, core: 2. Of those that a mesh axis runs over, the one named last changes fastest.
Arguments:
- block_inverse: bfloat16 [98304, 4096], P(('region', 'sub')), may hold values from -0.75 to 0.75
- probes: bfloat16 [98304, 4096], P(('region', 'sub')), may hold values from -6 to 6
- coupling: bfloat16 [16384, 32768], P(('region', 'sub')), may hold values from -0.25 to 0.25
- columns: int32 [16384, 8], P(('region', 'sub')), may hold values from 0 to 383
- residual: float32 [1048576], P(('region', 'sub')), may hold values from -6 to 6
Outputs:
- basis: float32 [1048576, 64], P(('region', 'sub'))
- correction: float32 [1048576], P(('region', 'sub'))
All inputs are finite; a program needn't handle non-finite values.
Results may differ from a plain program's by a relative error of at most 0.0058.
Values may be sent and summed in bfloat16 or wider, within the bound.
No kernel may reach another device: no remote copies, remote signals or barrier semaphores. Data moves between devices by JAX's collectives and lax.ppermute only.
A program may use at most 128 MiB of HBM per device.

v0:
```python
import jax
import jax.numpy as jnp
from jax import lax
from jax.sharding import PartitionSpec as P

BLOCK = 64
RANK = 64


def regroup_rows(run_pieces):
    return lax.all_to_all(run_pieces, "region", split_axis=0, concat_axis=0, tiled=True)


def per_device(block_inverse, probes, coupling, columns, residual):
    blocks_here = block_inverse.shape[0]
    interface_here = coupling.shape[0]
    couple_count = columns.shape[1]
    inverse_blocks = block_inverse.reshape(blocks_here, BLOCK, BLOCK)
    probe_blocks = probes.reshape(blocks_here, BLOCK, RANK)
    coupling_blocks = coupling.reshape(interface_here, couple_count, BLOCK, BLOCK)
    solved = jnp.einsum(
        "bij,bjk->bik", inverse_blocks, probe_blocks, preferred_element_type=jnp.float32
    ).astype(jnp.bfloat16)
    picked = solved[columns]
    pieces = jnp.einsum(
        "nkij,nkjr->nir", coupling_blocks, picked, preferred_element_type=jnp.float32
    ).astype(jnp.bfloat16)
    pieces = pieces.reshape(-1, RANK)
    regions = lax.axis_size("region")
    run_rows = pieces.shape[0] // regions
    run_pieces = pieces.reshape(regions, run_rows, RANK)
    total_rows = pieces.shape[0] * lax.axis_size("sub")
    owned_rows = regroup_rows(run_pieces)
    owned_rows = owned_rows.reshape(regions * run_rows, RANK)
    gram_local = jnp.dot(owned_rows.T, owned_rows, preferred_element_type=jnp.float32)
    owned_float = owned_rows.T.astype(jnp.float32)
    gram_total = lax.psum(gram_local, "sub")
    lower_factor = jnp.linalg.cholesky(gram_total)
    basis_t = jax.scipy.linalg.solve_triangular(lower_factor, owned_float, lower=True)
    coefficients = lax.psum(jnp.dot(basis_t, residual, precision=lax.Precision.HIGHEST), "sub")
    basis = jnp.sqrt(jnp.float32(total_rows)) * basis_t.T
    correction = jnp.sqrt(jnp.float32(total_rows) / RANK) * jnp.dot(
        basis_t.T, coefficients, precision=lax.Precision.HIGHEST
    )
    return (basis, correction)


def solution(mesh):
    placed = (
        P(("region", "sub"), None),
        P(("region", "sub"), None),
        P(("region", "sub"), None),
        P(("region", "sub"), None),
        P(("region", "sub")),
    )
    return jax.shard_map(
        per_device,
        mesh=mesh,
        in_specs=placed,
        out_specs=(P(("region", "sub"), None), P(("region", "sub"))),
        check_vma=False,
    )
```

profile of v0, /device:TPU:32, one launch (start us, length us, event | category | flops | bytes accessed | tf_op | source)
XLA Modules:
  0.0 326.1 jit_solution(5023297214685455433)
XLA Ops:
  0.6 0.0 copy-start
  0.6 3.4 %copy.10 = bf16[384,4096]{0,1:T(8,128)(2,1)S(1)} copy(bf16[384,4096]{1,0:T(8,128)(2,1)} %param.5) | data formatting | bytes 6291456 | tf_op args[0]
  4.1 9.5 %copy.12 = bf16[384,64,64]{2,1,0:T(8,128)(2,1)} copy(bf16[384,64,64]{0,2,1:T(8,128)(2,1)S(1)} %bitcast.49) | data formatting | bytes 6291456 | tf_op jit(solution)/shard_map/reshape | solution.py:18
  13.6 3.4 %copy.11 = bf16[384,4096]{0,1:T(8,128)(2,1)S(1)} copy(bf16[384,4096]{1,0:T(8,128)(2,1)} %param.6) | data formatting | bytes 6291456 | tf_op args[1]
  17.0 0.0 copy-start.1
  17.0 9.5 %copy.13 = bf16[384,64,64]{2,1,0:T(8,128)(2,1)} copy(bf16[384,64,64]{0,2,1:T(8,128)(2,1)S(1)} %bitcast.50) | data formatting | bytes 6291456 | tf_op jit(solution)/shard_map/reshape | solution.py:19
  26.5 0.0 copy-done.1
  26.5 0.1 copy.14
  26.6 0.1 reshape.32
  26.7 11.3 %reshape.28 = bf16[64,8,64,64]{3,2,1,0:T(8,128)(2,1)} reshape(bf16[64,32768]{1,0:T(8,128)(2,1)} %param.7) | data formatting | bytes 8388608 | tf_op jit(solution)/shard_map/reshape | solution.py:20
  38.1 9.1 %convolution_convert_fusion = bf16[384,64,64]{2,1,0:T(8,128)(2,1)} fusion(bf16[384,64,64]{2,1,0:T(8,128)(2,1)} %copy.12, bf16[384,64,64]{2,1,0:T(8,128)(2,1)} %copy.13), kind=kOutput, calls=%fused_computation.1 | convolution fusion | flops 202899456 | bytes 9437184 | tf_op jit(solution)/shard_map/bij,bjk->bik/dot_general | solution.py:21
  47.1 22.6 %gather_fusion = bf16[512,64,64]{2,1,0:T(8,128)(2,1)} fusion(bf16[384,64,64]{2,1,0:T(8,128)(2,1)} %convolution_convert_fusion, s32[1024]{0:T(1024)S(1)} %pad_clamp_fusion), kind=kCustom, calls=%fused_computation | custom fusion | bytes 8390656 | tf_op jit(solution)/shard_map/gather | solution.py:24
  69.7 8.2 %fusion = bf16[64,64,64]{1,2,0:T(8,128)(2,1)S(1)} fusion(bf16[64,8,64,64]{3,2,1,0:T(8,128)(2,1)} %bitcast.48, bf16[64,8,64,64]{3,2,1,0:T(8,128)(2,1)} %reshape.28), kind=kOutput, calls=%fused_computation.3 | convolution fusion | flops 268697600 | bytes 8912896 | tf_op jit(solution)/shard_map/nkij,nkjr->nir/dot_general | solution.py:25
  77.9 0.7 copy.16
  78.6 0.6 reshape_reshape.3
  79.2 0.2 copy.17
  79.4 14.5 %all_to_all.5 = bf16[8,512,64]{1,2,0:T(8,128)(2,1)S(1)} all-to-all(bf16[8,512,64]{1,2,0:T(8,128)(2,1)S(1)} %copy.17), channel_id=1, replica_groups=mesh['region'=8,'sub'=32] {'region'}, dimensions={0} | all-to-all | bytes 1048576 | tf_op jit(solution)/shard_map/all_to_all | solution.py:11
  93.9 0.3 convolution_bitcast_fusion
  94.1 140.7 %psum.14 = f32[64,64]{0,1:T(8,128)S(1)} all-reduce(f32[64,64]{0,1:T(8,128)S(1)} %convolution_bitcast_fusion), channel_id=1, replica_groups=mesh['region'=8,'sub'=32] {'sub'}, use_global_device_ids=true, to_apply=%region_0.0 | all-reduce | flops 4096 | bytes 32768 | tf_op jit(solution)/shard_map/psum | solution.py:37
  234.8 0.1 copy.19
  234.9 5.8 %cholesky.16 = f32[64,64]{1,0:T(8,128)S(1)} custom-call(f32[64,64]{1,0:T(8,128)S(1)} %fusion.6), custom_call_target="Cholesky" | custom-call | tf_op jit(solution)/shard_map/jit(cholesky)/cholesky | solution.py:38
  240.8 0.6 compare_reduce_fusion
  241.4 0.7 fusion.3
  242.1 4.9 %custom-call.7 = f32[1,64,64]{1,2,0:T(8,128)S(1)} custom-call(f32[1,64,64]{2,1,0:T(8,128)S(1)} %fusion.3), custom_call_target="InvertDiagBlocksLowerTriangular" | custom-call | tf_op jit(solution)/shard_map/jit(_solve_triangular)/triangular_solve | solution.py:39
  247.0 0.1 copy.25
  247.1 1.6 bitcast_multiply_fusion
  248.7 0.0 copy-done
  248.7 0.9 convolution_bitcast_fusion.1
  249.6 75.2 %psum.15 = f32[64]{0:T(128)S(1)} all-reduce(f32[64]{0:T(128)S(1)} %convolution_bitcast_fusion.1), channel_id=1, replica_groups=mesh['region'=8,'sub'=32] {'sub'}, use_global_device_ids=true, to_apply=%region_3.4 | all-reduce | flops 64 | bytes 512 | tf_op jit(solution)/shard_map/psum | solution.py:40
  324.8 0.7 fusion.1
  325.4 0.6 broadcast_multiply_fusion
  (4 shorter events, 0.1 us)
Async XLA Ops:
  0.6 248.0 %copy-start = (f32[4096]{0:T(1024)S(1)}, f32[4096]{0:T(1024)}, u32[]{:S(2)}) copy-start(f32[4096]{0:T(1024)} %param.9) | copy-start | bytes 49156
  17.0 9.5 %copy-start.1 = (s32[64,8]{0,1:T(8,128)S(1)}, s32[64,8]{0,1:T(8,128)}, u32[]{:S(2)}) copy-start(s32[64,8]{0,1:T(8,128)} %param.8) | copy-start | bytes 6148
where the time goes:
time: 327 us; the launch traced here: 326 us
  blocking collectives  230 us (70%)
  local copies, waits for them, and re-layouts  61.6 us (19%)
  matrix products  20.7 us (6%)
  other arithmetic  12.7 us (4%)
    psum x1, blocking collectives, per_device(): gram_total = lax.psum(gram_local, 'sub')  141 us
    psum x1, blocking collectives, per_device(): lax.psum(jnp.dot(basis_t, residual, precision=lax.Precision.HIGHEST), 'sub')  75.2 us
    gather x1, local copies, waits for them, and re-layouts, per_device(): picked = solved[columns]  22.6 us
    all_to_all x1, blocking collectives, regroup_rows(): lax.all_to_all(run_pieces, 'region', split_axis=0, concat_axis=0, tiled=T...  14.5 us
    reshape x1, local copies, waits for them, and re-layouts, per_device(): coupling.reshape(interface_here, couple_count, BLOCK, BLOCK)  11.3 us
    reshape x1, local copies, waits for them, and re-layouts, per_device(): probe_blocks = probes.reshape(blocks_here, BLOCK, RANK)  9.51 us
    reshape x1, local copies, waits for them, and re-layouts, per_device(): inverse_blocks = block_inverse.reshape(blocks_here, BLOCK, BLOCK)  9.5 us
    dot_general x1, matrix products, per_device(): jnp.einsum('bij,bjk->bik', inverse_blocks, probe_blocks, preferred_elemen...  9.05 us

commit v1 on v0

v1 whole, which is shorter than its diff:
```python
import functools
import math

import jax
import jax.numpy as jnp
from jax import lax
from jax.experimental import pallas as pl
from jax.experimental.pallas import tpu as pltpu
from jax.sharding import PartitionSpec as P

BLOCK = 64
RANK = 64
ROW = BLOCK * BLOCK
MIB = 2**20


def halves(x, y):
    even = jnp.concatenate([x[:, :BLOCK], y[:, :BLOCK]], axis=1)
    odd = jnp.concatenate([x[:, BLOCK:], y[:, BLOCK:]], axis=1)
    return even, odd


def spread(src, r0, c0, r1, c1, dst, base):
    for p in range(BLOCK // 2):
        x = src[pl.ds(r0, 16), pl.ds(c0 + 128 * p, 128)]
        y = src[pl.ds(r1, 16), pl.ds(c1 + 128 * p, 128)]
        even, odd = halves(x, y)
        dst[pl.ds(base + 32 * p, 16), :] = even.astype(jnp.float32)
        dst[pl.ds(base + 32 * p + 16, 16), :] = odd.astype(jnp.float32)


def pieces_kernel(cols_ref, inv_ref, prb_ref, cpl_ref, out_ref, inv_v, prb_v, cpl_v, stage_a, stage_p, stage_c, solved, sem):
    nb, ni = inv_ref.shape[0], cpl_ref.shape[0]
    kb = cpl_ref.shape[1] // ROW

    def interior_copies(g):
        rows = pl.ds(pl.multiple_of(g * 32, 32), 32)
        return (
            pltpu.make_async_copy(inv_ref.at[rows], inv_v.at[rows], sem.at[0, g]),
            pltpu.make_async_copy(prb_ref.at[rows], prb_v.at[rows], sem.at[1, g]),
        )

    def coupling_copy(g):
        rows = pl.ds(pl.multiple_of(g * 16, 16), 16)
        return pltpu.make_async_copy(cpl_ref.at[rows], cpl_v.at[rows], sem.at[2, g])

    for g in range(nb // 32):
        for copy in interior_copies(g):
            copy.start()
    for g in range(ni // 16):
        coupling_copy(g).start()
    low = lax.broadcasted_iota(jnp.int32, (BLOCK, 128), 1) < BLOCK

    def solve_group(g, carry):
        for copy in interior_copies(g):
            copy.wait()
        r0 = pl.multiple_of(g * 32, 32)
        spread(inv_v, r0, 0, r0 + 16, 0, stage_a, 0)
        spread(prb_v, r0, 0, r0 + 16, 0, stage_p, 0)
        for u in range(16):
            lhs = stage_a[pl.ds(u, BLOCK, stride=16), :].astype(jnp.bfloat16)
            prb = stage_p[pl.ds(u, BLOCK, stride=16), :]
            rhs = jnp.concatenate([jnp.where(low, prb, 0.0), jnp.where(low, 0.0, prb)], axis=0)
            both = jnp.dot(lhs, rhs.astype(jnp.bfloat16), preferred_element_type=jnp.float32)
            both = both.astype(jnp.bfloat16)
            solved[r0 + u] = both
            solved[r0 + 16 + u] = jnp.concatenate([both[:, BLOCK:], both[:, :BLOCK]], axis=1)
        return carry

    lax.fori_loop(0, nb // 32, solve_group, 0)

    def couple_group(g, carry):
        coupling_copy(g).wait()
        r0 = pl.multiple_of(g * 16, 16)
        for kp in range(kb // 2):
            spread(cpl_v, r0, 2 * ROW * kp, r0, 2 * ROW * kp + ROW, stage_c, 16 * BLOCK * kp)
        for up in range(8):
            two = []
            for u in (2 * up, 2 * up + 1):
                lhs = [stage_c[pl.ds(16 * BLOCK * kp + u, BLOCK, stride=16), :].astype(jnp.bfloat16) for kp in range(kb // 2)]
                rhs = [solved[cols_ref[(r0 + u) * kb + k]] for k in range(kb)]
                two.append(jnp.dot(jnp.concatenate(lhs, axis=1), jnp.concatenate(rhs, axis=0), preferred_element_type=jnp.float32))
            turned = jnp.transpose(jnp.concatenate(two, axis=0), (1, 0))[:RANK].astype(jnp.bfloat16)
            out_ref[2 * g + up // 4, :, (up % 4) * 128 : (up % 4) * 128 + 128] = turned
        return carry

    lax.fori_loop(0, ni // 16, couple_group, 0)


def turned_pieces(block_inverse, probes, coupling, columns, regions):
    nb, ni = block_inverse.shape[0], coupling.shape[0]
    any_place = pl.BlockSpec(memory_space=pl.ANY)
    return pl.pallas_call(
        pieces_kernel,
        out_shape=jax.ShapeDtypeStruct((regions, RANK, ni * BLOCK // regions), jnp.bfloat16),
        in_specs=[pl.BlockSpec(memory_space=pltpu.SMEM), any_place, any_place, any_place],
        out_specs=pl.BlockSpec(memory_space=pltpu.VMEM),
        scratch_shapes=[
            pltpu.VMEM(block_inverse.shape, jnp.bfloat16),
            pltpu.VMEM(probes.shape, jnp.bfloat16),
            pltpu.VMEM(coupling.shape, jnp.bfloat16),
            pltpu.VMEM((16 * BLOCK, 128), jnp.float32),
            pltpu.VMEM((16 * BLOCK, 128), jnp.float32),
            pltpu.VMEM((64 * BLOCK, 128), jnp.float32),
            pltpu.VMEM((nb, BLOCK, 128), jnp.bfloat16),
            pltpu.SemaphoreType.DMA((3, nb // 32)),
        ],
        compiler_params=pltpu.CompilerParams(vmem_limit_bytes=60 * MIB),
    )(columns.reshape(-1), block_inverse, probes, coupling)


NT = (((1,), (1,)), ((), ()))


def three_parts(x):
    high = x.astype(jnp.bfloat16)
    rest = x - high.astype(jnp.float32)
    middle = rest.astype(jnp.bfloat16)
    low = (rest - middle.astype(jnp.float32)).astype(jnp.bfloat16)
    return jnp.concatenate([high, middle, low], axis=0)


def gram_kernel(rows_ref, res_ref, out_ref):
    regions, rank, run = rows_ref.shape
    gram = jnp.zeros((rank, rank), jnp.float32)
    moment = jnp.zeros((3, rank), jnp.float32)
    for r in range(regions):
        y = rows_ref[r]
        gram += lax.dot_general(y, y, NT, preferred_element_type=jnp.float32)
        parts = three_parts(res_ref[:, r * run : (r + 1) * run])
        moment += lax.dot_general(parts, y, NT, preferred_element_type=jnp.float32)
    half = rank // 2
    out_ref[:half, :] = jnp.concatenate([gram[:half], gram[half:]], axis=1)
    row = moment[0:1] + moment[1:2] + moment[2:3]
    row = jnp.concatenate([row, jnp.zeros_like(row)], axis=1)
    out_ref[half:, :] = jnp.broadcast_to(row, (8, 2 * rank))


def finish_kernel(total_rows, sum_ref, rows_ref, basis_ref, corr_ref, basis_v, sem):
    regions, rank, run = rows_ref.shape
    half = rank // 2
    packed = sum_ref[:half, :]
    gram = jnp.concatenate([packed[:, :rank], packed[:, rank:]], axis=0)
    moment = sum_ref[half : half + 1, :rank]
    row_at = lax.broadcasted_iota(jnp.int32, (rank, 2 * rank), 0)
    lane_at = lax.broadcasted_iota(jnp.int32, (rank, 2 * rank), 1)
    one = (lane_at == row_at + rank).astype(jnp.float32)
    m = jnp.concatenate([gram, jnp.zeros_like(gram)], axis=1) + one
    for k in range(rank):
        pivot_row = m[k : k + 1, :]
        inverse = 1.0 / pivot_row[:, k : k + 1]
        column = jnp.broadcast_to(m[:, k : k + 1], (rank, 2 * rank))
        factor = jnp.where(row_at > k, column, 0.0) * inverse
        m = m - factor * pivot_row
    diagonal = jnp.sum(jnp.where(row_at == lane_at, m, 0.0), axis=1, keepdims=True)
    lower_inverse = m[:, rank:] * (1.0 / jnp.sqrt(diagonal))
    coefficients = jnp.sum(lower_inverse * moment, axis=1, keepdims=True)
    scale = math.sqrt(total_rows)
    weights = three_parts(lower_inverse * scale)
    weights = weights[: 2 * rank]
    shrink = 1.0 / math.sqrt(rank)

    def copy_out(r):
        cols = pl.ds(r * run, run)
        return pltpu.make_async_copy(basis_v.at[:, cols], basis_ref.at[:, cols], sem.at[r])

    for r in range(regions):
        q = jnp.dot(weights, rows_ref[r], preferred_element_type=jnp.float32)
        q = q[:rank] + q[rank:]
        basis_v[:, r * run : (r + 1) * run] = q
        copy_out(r).start()
        corr_ref[:, r * run : (r + 1) * run] = jnp.sum(q * (coefficients * shrink), axis=0, keepdims=True)
    for r in range(regions):
        copy_out(r).wait()


def per_device(block_inverse, probes, coupling, columns, residual):
    regions, subs = lax.axis_size("region"), lax.axis_size("sub")
    rows_here = residual.shape[0]
    in_vmem = pl.BlockSpec(memory_space=pltpu.VMEM)
    pieces = turned_pieces(block_inverse, probes, coupling, columns, regions)
    owned = lax.all_to_all(pieces, "region", split_axis=0, concat_axis=0, tiled=True)
    total = pl.pallas_call(
        gram_kernel,
        out_shape=jax.ShapeDtypeStruct((RANK // 2 + 8, 2 * RANK), jnp.float32),
        in_specs=[in_vmem, in_vmem],
        out_specs=in_vmem,
    )(owned, residual.reshape(1, rows_here))
    for step in (8, 24, 1, 6, 2):
        total = total + lax.ppermute(total, "sub", [(i, i ^ step) for i in range(subs)])
    basis_t, correction = pl.pallas_call(
        functools.partial(finish_kernel, rows_here * subs),
        out_shape=(
            jax.ShapeDtypeStruct((RANK, rows_here), jnp.float32),
            jax.ShapeDtypeStruct((1, rows_here), jnp.float32),
        ),
        in_specs=[in_vmem, in_vmem],
        out_specs=(pl.BlockSpec(memory_space=pl.ANY), in_vmem),
        scratch_shapes=[pltpu.VMEM((RANK, rows_here), jnp.float32), pltpu.SemaphoreType.DMA((regions,))],
    )(total, owned)
    return basis_t.T, correction.reshape(rows_here)


def solution(mesh):
    blocks = P(("region", "sub"), None)
    rows = P(("region", "sub"))
    return jax.shard_map(
        per_device,
        mesh=mesh,
        in_specs=(blocks, blocks, blocks, blocks, rows),
        out_specs=(blocks, rows),
        check_vma=False,
    )
```

time: 327 us -> 73.5 us (0.22)
  blocking collectives: 230 us -> 14.8 us
  local copies, waits for them, and re-layouts: 61.6 us -> 1.44 us
  Pallas kernels: 0 us -> 29.4 us
  matrix products: 20.7 us -> 0 us
  starting transfers between devices: 0 us -> 13.6 us
  other arithmetic: 12.7 us -> 1.35 us
  waiting for transfers between devices: 0 us -> 11.1 us
    psum x2 -> x0, blocking collectives: 216 us -> none  [the longest x1 141 us: per_device(): gram_total = lax.psum(gram_local, 'sub')]
    reshape x4 -> x1, local copies, waits for them, and re-layouts: 30.4 us -> 0.67 us  [turned_pieces(): columns.reshape(-1)]
    pallas_call x0 -> x3, Pallas kernels: none -> 29.4 us  [the longest x1 16.1 us: turned_pieces(): pl.pallas_call(pieces_kernel, out_shape=jax.ShapeDtypeStruct((regions, RA...]
    gather x1 -> x0, local copies, waits for them, and re-layouts: 22.6 us -> none  [per_device(): picked = solved[columns]]
    dot_general x5 -> x0, matrix products: 19.1 us -> none  [the longest x1 9.05 us: per_device(): jnp.einsum('bij,bjk->bik', inverse_blocks, probe_blocks, preferred_elemen...]
    ppermute x0 -> x5, starting transfers between devices: none -> 13.6 us  [per_device(): lax.ppermute(total, 'sub', [(i, i ^ step) for i in range(subs)])]
    another operation x5 -> x0, other arithmetic: 12.1 us -> none  [the longest x3 6.52 us: per_device(): lower_factor = jnp.linalg.cholesky(gram_total)]
    ppermute x0 -> x5, waiting for transfers between devices: none -> 11.1 us  [per_device(): lax.ppermute(total, 'sub', [(i, i ^ step) for i in range(subs)])]
  transfers between devices with their start and end apart: 0 -> 5, of which waited for: 0 -> 5; matrix products, arithmetic and copies ran while one was open for 0% -> 0% of each run, Pallas kernels for 0% -> 0%
where the time goes in v1:
time: 73.5 us; the launch traced here: 72.2 us
  Pallas kernels  29.4 us (40%)
  blocking collectives  14.8 us (20%)
  starting transfers between devices  13.6 us (19%)
  waiting for transfers between devices  11.1 us (15%)
  local copies, waits for them, and re-layouts  1.44 us (2%)
  other arithmetic  1.35 us (2%)
    pallas_call x1, Pallas kernels, turned_pieces(): pl.pallas_call(pieces_kernel, out_shape=jax.ShapeDtypeStruct((regions, RA...  16.1 us
    all_to_all x1, blocking collectives, per_device(): lax.all_to_all(pieces, 'region', split_axis=0, concat_axis=0, tiled=True)  14.8 us
    ppermute x5, starting transfers between devices, per_device(): lax.ppermute(total, 'sub', [(i, i ^ step) for i in range(subs)])  13.6 us
    pallas_call x1, Pallas kernels, per_device(): pl.pallas_call(functools.partial(finish_kernel, rows_here * subs), out_sh...  11.2 us
    ppermute x5, waiting for transfers between devices, per_device(): lax.ppermute(total, 'sub', [(i, i ^ step) for i in range(subs)])  11.1 us
    pallas_call x1, Pallas kernels, per_device(): pl.pallas_call(gram_kernel, out_shape=jax.ShapeDtypeStruct((RANK // 2 + 8...  2.12 us
  transfers between devices with their start and end apart: 5, of which 5 were waited for; matrix products, arithmetic and copies ran while one was open for 0% of the time, Pallas kernels for 0%

profile of v1, /device:TPU:32, one launch (start us, length us, event | category | flops | bytes accessed | tf_op | source)
XLA Modules:
  0.0 72.2 jit_solution(9297968817286622525)
XLA Ops:
  0.6 0.8 %copy.7 = s32[64,8]{1,0:T(8,128)S(1)} copy(s32[64,8]{0,1:T(8,128)} %param.8) | data formatting | bytes 4096 | tf_op args[3]
  1.4 0.7 reshape.13.cols_ref
  2.1 16.1 %shard_map.68 = bf16[8,64,512]{2,1,0:T(8,128)(2,1)} custom-call(s32[512]{0:T(512)} %reshape.13.cols_ref, bf16[384,4096]{1,0:T(8,128)(2,1)} %inv_ref.1, bf16[384,4096]{1,0:T(8,128)(2,1)} %prb_ref.1, bf16[64,32768]{1,0:T(8,128)(2,1)} %cpl_ref.1), custom_call_target="tpu_custom_call" | custom-call | tf_op jit(solution)/shard_map/pallas_call | solution.py:93
  18.1 14.8 %all_to_all.5.rows_ref = bf16[8,64,512]{2,1,0:T(8,128)(2,1)} all-to-all(bf16[8,64,512]{2,1,0:T(8,128)(2,1)} %shard_map.68), channel_id=1, replica_groups=mesh['region'=8,'sub'=32] {'region'}, dimensions={0} | all-to-all | bytes 1048576 | tf_op jit(solution)/shard_map/all_to_all | solution.py:182
  32.9 2.1 %shard_map.69 = f32[40,128]{1,0:T(8,128)} custom-call(bf16[8,64,512]{2,1,0:T(8,128)(2,1)} %all_to_all.5.rows_ref, f32[1,4096]{1,0:T(1,128)} %bitcast.3), custom_call_target="tpu_custom_call" | custom-call | tf_op jit(solution)/shard_map/pallas_call | solution.py:183
  35.1 1.6 %collective-permute-start = (f32[40,128]{1,0:T(8,128)}, f32[40,128]{1,0:T(8,128)S(1)}, u32[]{:S(2)}, u32[]{:S(2)}) collective-permute-start(f32[40,128]{1,0:T(8,128)} %shard_map.69), channel_id=1, source_target_pairs={{0,8},{1,9},{2,10},{3,11},{4,12},{5,13},{6,14},{7,15},{8,0},{9,1},... | collective-permute-start | bytes 61448 | tf_op jit(solution)/shard_map/ppermute | solution.py:190
  36.6 2.4 %collective-permute-done = f32[40,128]{1,0:T(8,128)S(1)} collective-permute-done((f32[40,128]{1,0:T(8,128)}, f32[40,128]{1,0:T(8,128)S(1)}, u32[]{:S(2)}, u32[]{:S(2)}) %collective-permute-start) | collective-permute-done | bytes 20512 | tf_op jit(solution)/shard_map/ppermute | solution.py:190
  39.1 0.7 %add.15 = f32[40,128]{1,0:T(8,128)S(1)} add(f32[40,128]{1,0:T(8,128)} %shard_map.69, f32[40,128]{1,0:T(8,128)S(1)} %collective-permute-done) | non-fusion elementwise | flops 5120 | bytes 61440 | tf_op jit(solution)/shard_map/add | solution.py:190
  39.8 3.0 %collective-permute-start.1 = (f32[40,128]{1,0:T(8,128)S(1)}, f32[40,128]{1,0:T(8,128)S(1)}, u32[]{:S(2)}, u32[]{:S(2)}) collective-permute-start(f32[40,128]{1,0:T(8,128)S(1)} %add.15), channel_id=1, source_target_pairs={{0,24},{1,25},{2,26},{3,27},{4,28},{5,29},{6,30},{7,31},{8,16},{9,... | collective-permute-start | bytes 61448 | tf_op jit(solution)/shard_map/ppermute | solution.py:190
  42.8 2.0 %collective-permute-done.1 = f32[40,128]{1,0:T(8,128)S(1)} collective-permute-done((f32[40,128]{1,0:T(8,128)S(1)}, f32[40,128]{1,0:T(8,128)S(1)}, u32[]{:S(2)}, u32[]{:S(2)}) %collective-permute-start.1) | collective-permute-done | bytes 20512 | tf_op jit(solution)/shard_map/ppermute | solution.py:190
  44.8 1.6 %collective-permute-start.2 = (f32[40,128]{1,0:T(8,128)S(1)}, f32[40,128]{1,0:T(8,128)S(1)}, u32[]{:S(2)}, u32[]{:S(2)}) collective-permute-start(f32[40,128]{1,0:T(8,128)S(1)} %add.16), channel_id=1, source_target_pairs={{0,1},{1,0},{2,3},{3,2},{4,5},{5,4},{6,7},{7,6},{8,9},{9,8},{10,11... | collective-permute-start | bytes 61448 | tf_op jit(solution)/shard_map/ppermute | solution.py:190
  46.3 2.2 %collective-permute-done.2 = f32[40,128]{1,0:T(8,128)S(1)} collective-permute-done((f32[40,128]{1,0:T(8,128)S(1)}, f32[40,128]{1,0:T(8,128)S(1)}, u32[]{:S(2)}, u32[]{:S(2)}) %collective-permute-start.2) | collective-permute-done | bytes 20512 | tf_op jit(solution)/shard_map/ppermute | solution.py:190
  48.6 5.4 %collective-permute-start.3 = (f32[40,128]{1,0:T(8,128)S(1)}, f32[40,128]{1,0:T(8,128)S(1)}, u32[]{:S(2)}, u32[]{:S(2)}) collective-permute-start(f32[40,128]{1,0:T(8,128)S(1)} %add.17), channel_id=1, source_target_pairs={{0,6},{1,7},{2,4},{3,5},{4,2},{5,3},{6,0},{7,1},{8,14},{9,15},{10,... | collective-permute-start | bytes 61448 | tf_op jit(solution)/shard_map/ppermute | solution.py:190
  54.0 1.8 %collective-permute-done.3 = f32[40,128]{1,0:T(8,128)S(1)} collective-permute-done((f32[40,128]{1,0:T(8,128)S(1)}, f32[40,128]{1,0:T(8,128)S(1)}, u32[]{:S(2)}, u32[]{:S(2)}) %collective-permute-start.3) | collective-permute-done | bytes 20512 | tf_op jit(solution)/shard_map/ppermute | solution.py:190
  55.7 2.0 %collective-permute-start.4 = (f32[40,128]{1,0:T(8,128)S(1)}, f32[40,128]{1,0:T(8,128)S(1)}, u32[]{:S(2)}, u32[]{:S(2)}) collective-permute-start(f32[40,128]{1,0:T(8,128)S(1)} %add.18), channel_id=1, source_target_pairs={{0,2},{1,3},{2,0},{3,1},{4,6},{5,7},{6,4},{7,5},{8,10},{9,11},{10,... | collective-permute-start | bytes 61448 | tf_op jit(solution)/shard_map/ppermute | solution.py:190
  57.7 2.7 %collective-permute-done.4 = f32[40,128]{1,0:T(8,128)S(1)} collective-permute-done((f32[40,128]{1,0:T(8,128)S(1)}, f32[40,128]{1,0:T(8,128)S(1)}, u32[]{:S(2)}, u32[]{:S(2)}) %collective-permute-start.4) | collective-permute-done | bytes 20512 | tf_op jit(solution)/shard_map/ppermute | solution.py:190
  60.4 0.6 add.19.sum_ref
  61.0 11.2 %shard_map.70 = (f32[64,4096]{1,0:T(8,128)}, f32[1,4096]{1,0:T(1,128)}) custom-call(f32[40,128]{1,0:T(8,128)} %add.19.sum_ref, bf16[8,64,512]{2,1,0:T(8,128)(2,1)} %all_to_all.5.rows_ref), custom_call_target="tpu_custom_call" | custom-call | tf_op jit(solution)/shard_map/pallas_call | solution.py:191
  (3 shorter events, 0.0 us)
Async XLA Ops:
  35.1 4.0 %collective-permute-start = (f32[40,128]{1,0:T(8,128)}, f32[40,128]{1,0:T(8,128)S(1)}, u32[]{:S(2)}, u32[]{:S(2)}) collective-permute-start(f32[40,128]{1,0:T(8,128)} %shard_map.69), channel_id=1, source_target_pairs={{0,8},{1,9},{2,10},{3,11},{4,12},{5,13},{6,14},{7,15},{8,0},{9,1},... | collective-permute-start | bytes 61448 | tf_op jit(solution)/shard_map/ppermute | solution.py:190
  39.8 5.0 %collective-permute-start.1 = (f32[40,128]{1,0:T(8,128)S(1)}, f32[40,128]{1,0:T(8,128)S(1)}, u32[]{:S(2)}, u32[]{:S(2)}) collective-permute-start(f32[40,128]{1,0:T(8,128)S(1)} %add.15), channel_id=1, source_target_pairs={{0,24},{1,25},{2,26},{3,27},{4,28},{5,29},{6,30},{7,31},{8,16},{9,... | collective-permute-start | bytes 61448 | tf_op jit(solution)/shard_map/ppermute | solution.py:190
  44.8 3.8 %collective-permute-start.2 = (f32[40,128]{1,0:T(8,128)S(1)}, f32[40,128]{1,0:T(8,128)S(1)}, u32[]{:S(2)}, u32[]{:S(2)}) collective-permute-start(f32[40,128]{1,0:T(8,128)S(1)} %add.16), channel_id=1, source_target_pairs={{0,1},{1,0},{2,3},{3,2},{4,5},{5,4},{6,7},{7,6},{8,9},{9,8},{10,11... | collective-permute-start | bytes 61448 | tf_op jit(solution)/shard_map/ppermute | solution.py:190
  48.6 7.2 %collective-permute-start.3 = (f32[40,128]{1,0:T(8,128)S(1)}, f32[40,128]{1,0:T(8,128)S(1)}, u32[]{:S(2)}, u32[]{:S(2)}) collective-permute-start(f32[40,128]{1,0:T(8,128)S(1)} %add.17), channel_id=1, source_target_pairs={{0,6},{1,7},{2,4},{3,5},{4,2},{5,3},{6,0},{7,1},{8,14},{9,15},{10,... | collective-permute-start | bytes 61448 | tf_op jit(solution)/shard_map/ppermute | solution.py:190
  55.7 4.7 %collective-permute-start.4 = (f32[40,128]{1,0:T(8,128)S(1)}, f32[40,128]{1,0:T(8,128)S(1)}, u32[]{:S(2)}, u32[]{:S(2)}) collective-permute-start(f32[40,128]{1,0:T(8,128)S(1)} %add.18), channel_id=1, source_target_pairs={{0,2},{1,3},{2,0},{3,1},{4,6},{5,7},{6,4},{7,5},{8,10},{9,11},{10,... | collective-permute-start | bytes 61448 | tf_op jit(solution)/shard_map/ppermute | solution.py:190

commit v2 on v1

v2 whole, which is shorter than its diff:
```python
import functools
import math

import jax
import jax.numpy as jnp
from jax import lax
from jax.experimental import pallas as pl
from jax.experimental.pallas import tpu as pltpu
from jax.sharding import PartitionSpec as P

BLOCK = 64
RANK = 64
ROW = BLOCK * BLOCK
MIB = 2**20
STEP = 8
NT = (((1,), (1,)), ((), ()))


def spread(src, r0, c0, r1, c1, dst, base, p):
    x = src[pl.ds(r0, 16), pl.ds(c0 + 128 * p, 128)]
    y = src[pl.ds(r1, 16), pl.ds(c1 + 128 * p, 128)]
    even = jnp.concatenate([x[:, :BLOCK], y[:, :BLOCK]], axis=1).astype(jnp.float32)
    odd = jnp.concatenate([x[:, BLOCK:], y[:, BLOCK:]], axis=1).astype(jnp.float32)
    for h in range(2):
        at = base + 8 * BLOCK * h + 16 * p
        dst[pl.ds(at, 8), :] = even[8 * h : 8 * h + 8]
        dst[pl.ds(at + 8, 8), :] = odd[8 * h : 8 * h + 8]

def gathered(stage, base, u):
    return stage[pl.ds(base + u // 8 * 8 * BLOCK + u % 8, BLOCK, stride=8), :]

def pieces_kernel(cols_hbm, inv_ref, prb_ref, cpl_ref, out_ref, cols, inv_v, prb_v, cpl_v, a0, a1, p0, p1, c0, c1, solved, sem, cols_sem):
    nb, ni = inv_ref.shape[0], cpl_ref.shape[0]
    kb = cpl_ref.shape[1] // ROW
    groups, cgroups = nb // 32, ni // 16

    def interior_copies(g):
        rows = pl.ds(pl.multiple_of(g * 32, 32), 32)
        return (
            pltpu.make_async_copy(inv_ref.at[rows], inv_v.at[rows], sem.at[0, g]),
            pltpu.make_async_copy(prb_ref.at[rows], prb_v.at[rows], sem.at[1, g]),
        )

    def coupling_copy(g):
        rows = pl.ds(pl.multiple_of(g * 16, 16), 16)
        return pltpu.make_async_copy(cpl_ref.at[rows], cpl_v.at[rows], sem.at[2, g])

    cols_copy = pltpu.make_async_copy(cols_hbm, cols, cols_sem)
    for copy in interior_copies(0):
        copy.start()
    cols_copy.start()
    for g in range(1, groups):
        for copy in interior_copies(g):
            copy.start()
    for g in range(cgroups):
        coupling_copy(g).start()
    low = lax.broadcasted_iota(jnp.int32, (BLOCK, 128), 1) < BLOCK

    def solve_spread(g, sa, sp, p):
        r0 = pl.multiple_of(g * 32, 32)
        spread(inv_v, r0, 0, r0 + 16, 0, sa, 0, p)
        spread(prb_v, r0, 0, r0 + 16, 0, sp, 0, p)

    def solve(g, sa, sp, u):
        r0 = g * 32
        lhs = gathered(sa, 0, u).astype(jnp.bfloat16)
        prb = gathered(sp, 0, u)
        rhs = jnp.concatenate([jnp.where(low, prb, 0.0), jnp.where(low, 0.0, prb)], axis=0)
        both = jnp.dot(lhs, rhs.astype(jnp.bfloat16), preferred_element_type=jnp.float32)
        both = both.astype(jnp.bfloat16)
        solved[r0 + u] = both
        solved[r0 + 16 + u] = jnp.concatenate([both[:, BLOCK:], both[:, :BLOCK]], axis=1)

    def couple_spread(g, sc, q):
        kp, p = q // 32, q % 32
        r0 = pl.multiple_of(g * 16, 16)
        spread(cpl_v, r0, 2 * ROW * kp, r0, 2 * ROW * kp + ROW, sc, 16 * BLOCK * kp, p)

    def couple(g, sc, up):
        two = []
        for u in (2 * up, 2 * up + 1):
            lhs = [gathered(sc, 16 * BLOCK * kp, u).astype(jnp.bfloat16) for kp in range(kb // 2)]
            rhs = [solved[cols[k, g * 16 + u]] for k in range(kb)]
            two.append(jnp.dot(jnp.concatenate(lhs, axis=1), jnp.concatenate(rhs, axis=0), preferred_element_type=jnp.float32))
        turned = jnp.transpose(jnp.concatenate(two, axis=0).astype(jnp.bfloat16), (1, 0))[:RANK]
        out_ref[2 * g + up // 4, :, (up % 4) * 128 : (up % 4) * 128 + 128] = turned

    def wait(g):
        for copy in interior_copies(g):
            copy.wait()

    def solve_beside(g, sa, sp, na, np_):
        wait(g + 1)
        for u in range(16):
            solve(g, sa, sp, u)
            for p in (2 * u, 2 * u + 1):
                solve_spread(g + 1, na, np_, p)

    wait(0)
    for p in range(32):
        solve_spread(0, a0, p0, p)

    def two_groups(t, carry):
        solve_beside(2 * t, a0, p0, a1, p1)
        solve_beside(2 * t + 1, a1, p1, a0, p0)
        return carry

    lax.fori_loop(0, groups // 2 - 1, two_groups, 0)
    solve_beside(groups - 2, a0, p0, a1, p1)
    coupling_copy(0).wait()
    for u in range(16):
        solve(groups - 1, a1, p1, u)
        for q in range(8 * u, 8 * u + 8):
            couple_spread(0, c0, q)
    cols_copy.wait()
    for g in range(cgroups):
        here, there = (c0, c1) if g % 2 == 0 else (c1, c0)
        if g + 1 < cgroups:
            coupling_copy(g + 1).wait()
        for up in range(8):
            couple(g, here, up)
            if g + 1 < cgroups:
                for q in range(16 * up, 16 * up + 16):
                    couple_spread(g + 1, there, q)


def turned_pieces(block_inverse, probes, coupling, columns, regions):
    nb, ni = block_inverse.shape[0], coupling.shape[0]
    any_place = pl.BlockSpec(memory_space=pl.ANY)
    stage = pltpu.VMEM((16 * BLOCK, 128), jnp.float32)
    big = pltpu.VMEM((64 * BLOCK, 128), jnp.float32)
    return pl.pallas_call(
        pieces_kernel,
        out_shape=jax.ShapeDtypeStruct((regions, RANK, ni * BLOCK // regions), jnp.bfloat16),
        in_specs=[any_place] * 4,
        out_specs=pl.BlockSpec(memory_space=pltpu.VMEM),
        scratch_shapes=[
            pltpu.SMEM(columns.shape[::-1], jnp.int32),
            pltpu.VMEM(block_inverse.shape, jnp.bfloat16),
            pltpu.VMEM(probes.shape, jnp.bfloat16),
            pltpu.VMEM(coupling.shape, jnp.bfloat16),
            stage, stage, stage, stage, big, big,
            pltpu.VMEM((nb, BLOCK, 128), jnp.bfloat16),
            pltpu.SemaphoreType.DMA((3, nb // 32)),
            pltpu.SemaphoreType.DMA(()),
        ],
        compiler_params=pltpu.CompilerParams(vmem_limit_bytes=58 * MIB),
    )(columns.T, block_inverse, probes, coupling)


def three_parts(x):
    high = x.astype(jnp.bfloat16)
    rest = x - high.astype(jnp.float32)
    middle = rest.astype(jnp.bfloat16)
    low = (rest - middle.astype(jnp.float32)).astype(jnp.bfloat16)
    return jnp.concatenate([high, middle, low], axis=0)


def gram_kernel(rows_ref, res_ref, out_ref):
    regions, rank, run = rows_ref.shape
    gram = jnp.zeros((rank, rank), jnp.float32)
    moment = jnp.zeros((3, rank), jnp.float32)
    for r in range(regions):
        y = rows_ref[r]
        gram += lax.dot_general(y, y, NT, preferred_element_type=jnp.float32)
        parts = three_parts(res_ref[:, r * run : (r + 1) * run])
        moment += lax.dot_general(parts, y, NT, preferred_element_type=jnp.float32)
    half = rank // 2
    out_ref[:half, :] = jnp.concatenate([gram[:half], gram[half:]], axis=1)
    row = moment[0:1] + moment[1:2] + moment[2:3]
    row = jnp.concatenate([row, jnp.zeros_like(row)], axis=1)
    out_ref[half:, :] = jnp.broadcast_to(row, (8, 2 * rank))


def two_parts(x):
    high = x.astype(jnp.bfloat16)
    return jnp.concatenate([high, (x - high.astype(jnp.float32)).astype(jnp.bfloat16)], axis=0)


def inverse_lower(gram):
    rank = gram.shape[0]
    row_at = lax.broadcasted_iota(jnp.int32, (rank, 2 * rank), 0)
    lane_at = lax.broadcasted_iota(jnp.int32, (rank, 2 * rank), 1)
    rest = jnp.concatenate([gram, jnp.zeros_like(gram)], axis=1) + (lane_at == row_at + rank).astype(jnp.float32)
    done = []
    for k in range(0, rank, STEP):
        at = row_at[: rank - k]
        cols = [jnp.broadcast_to(rest[:, k + j : k + j + 1], rest.shape) for j in range(STEP)]
        rows = [rest[j : j + 1, :] for j in range(STEP)]
        pivots = []
        for j in range(STEP):
            pivot = cols[j][j : j + 1, :]
            pivots.append(pivot)
            factor = jnp.where(at > j, cols[j] * (1.0 / pivot), 0.0)
            for l in range(j + 1, STEP):
                cols[l] = cols[l] - factor * cols[l][j : j + 1, :]
                rows[l] = rows[l] - factor[l : l + 1, :] * rows[j]
            rest = rest - factor * rows[j]
        done.append(rest[:STEP, rank:] * lax.rsqrt(jnp.concatenate(pivots, axis=0)[:, :rank]))
        rest = rest[STEP:]
    return jnp.concatenate(done, axis=0)


def finish_kernel(total_rows, sum_ref, more_ref, rows_ref, basis_ref, corr_ref, basis_v, sem):
    regions, rank, run = rows_ref.shape
    half = rank // 2
    total = sum_ref[...] + more_ref[...]
    packed = total[:half]
    gram = jnp.concatenate([packed[:, :rank], packed[:, rank:]], axis=0)
    moment = total[half : half + 1, :rank]
    lower_inverse = inverse_lower(gram)
    coefficients = jnp.sum(lower_inverse * moment, axis=1, keepdims=True)
    weights = two_parts(lower_inverse * math.sqrt(total_rows))
    shrink = 1.0 / math.sqrt(rank)

    def copy_out(r):
        cols = pl.ds(r * run, run)
        return pltpu.make_async_copy(basis_v.at[:, cols], basis_ref.at[:, cols], sem.at[r])

    for r in range(regions):
        q = jnp.dot(weights, rows_ref[r], preferred_element_type=jnp.float32)
        q = q[:rank] + q[rank:]
        basis_v[:, r * run : (r + 1) * run] = q
        copy_out(r).start()
        corr_ref[:, r * run : (r + 1) * run] = jnp.sum(q * (coefficients * shrink), axis=0, keepdims=True)
    for r in range(regions):
        copy_out(r).wait()


def per_device(block_inverse, probes, coupling, columns, residual):
    regions, subs = lax.axis_size("region"), lax.axis_size("sub")
    rows_here = residual.shape[0]
    in_vmem = pl.BlockSpec(memory_space=pltpu.VMEM)
    pieces = turned_pieces(block_inverse, probes, coupling, columns, regions)
    owned = lax.all_to_all(pieces, "region", split_axis=0, concat_axis=0, tiled=True)
    total = pl.pallas_call(
        gram_kernel,
        out_shape=jax.ShapeDtypeStruct((RANK // 2 + 8, 2 * RANK), jnp.float32),
        in_specs=[in_vmem, in_vmem],
        out_specs=in_vmem,
        compiler_params=pltpu.CompilerParams(vmem_limit_bytes=16 * MIB),
    )(owned, residual.reshape(1, rows_here))
    more = jnp.zeros_like(total)
    for n, step in enumerate((8, 24, 1, 6, 2)):
        total = total + more if n else total
        more = lax.ppermute(total, "sub", [(i, i ^ step) for i in range(subs)])
    basis_t, correction = pl.pallas_call(
        functools.partial(finish_kernel, rows_here * subs),
        out_shape=(
            jax.ShapeDtypeStruct((RANK, rows_here), jnp.float32),
            jax.ShapeDtypeStruct((1, rows_here), jnp.float32),
        ),
        in_specs=[in_vmem, in_vmem, in_vmem],
        out_specs=(pl.BlockSpec(memory_space=pl.ANY), in_vmem),
        scratch_shapes=[pltpu.VMEM((RANK, rows_here), jnp.float32), pltpu.SemaphoreType.DMA((regions,))],
        compiler_params=pltpu.CompilerParams(vmem_limit_bytes=16 * MIB),
    )(total, more, owned)
    return basis_t.T, correction.reshape(rows_here)


def solution(mesh):
    blocks = P(("region", "sub"), None)
    rows = P(("region", "sub"))
    return jax.shard_map(
        per_device,
        mesh=mesh,
        in_specs=(blocks, blocks, blocks, blocks, rows),
        out_specs=(blocks, rows),
        check_vma=False,
    )
```

time: 73.5 us -> 55.9 us (0.76)
  Pallas kernels: 29.4 us -> 15 us
  local copies, waits for them, and re-layouts: 1.44 us -> 0.01 us
  other arithmetic: 1.35 us -> 0.02 us
    pallas_call x1, Pallas kernels: 11.2 us -> 3.62 us  [per_device(): pl.pallas_call(functools.partial(finish_kernel, rows_here * subs), out_sh...]
    pallas_call x1, Pallas kernels: 16.1 us -> 10.9 us  [turned_pieces(): pl.pallas_call(pieces_kernel, out_shape=jax.ShapeDtypeStruct((regions, RA...]
    pallas_call x1, Pallas kernels: 2.12 us -> 0.47 us  [per_device(): pl.pallas_call(gram_kernel, out_shape=jax.ShapeDtypeStruct((RANK // 2 + 8...]
    add x5 -> x4, other arithmetic: 1.35 us -> 0.02 us  [per_device(): total = total + more if n else total]
    unnamed x1 -> x2, local copies, waits for them, and re-layouts: 0.77 us -> 0.01 us
where the time goes in v2:
time: 55.9 us; the launch traced here: 54.8 us
  Pallas kernels  15 us (27%)
  blocking collectives  14.7 us (26%)
  starting transfers between devices  13 us (23%)
  waiting for transfers between devices  11.5 us (21%)
  between operations  0.66 us (1%)
    all_to_all x1, blocking collectives, per_device(): lax.all_to_all(pieces, 'region', split_axis=0, concat_axis=0, tiled=True)  14.7 us
    ppermute x5, starting transfers between devices, per_device(): more = lax.ppermute(total, 'sub', [(i, i ^ step) for i in range(subs)])  13 us
    ppermute x5, waiting for transfers between devices, per_device(): more = lax.ppermute(total, 'sub', [(i, i ^ step) for i in range(subs)])  11.5 us
    pallas_call x1, Pallas kernels, turned_pieces(): pl.pallas_call(pieces_kernel, out_shape=jax.ShapeDtypeStruct((regions, RA...  10.9 us
    pallas_call x1, Pallas kernels, per_device(): pl.pallas_call(functools.partial(finish_kernel, rows_here * subs), out_sh...  3.62 us
  transfers between devices with their start and end apart: 5, of which 5 were waited for; matrix products, arithmetic and copies ran while one was open for 0% of the time, Pallas kernels for 0%

profile of v2, /device:TPU:32, one launch (start us, length us, event | category | flops | bytes accessed | tf_op | source)
XLA Modules:
  0.0 54.8 jit_solution(10852594232340201595)
XLA Ops:
  0.6 0.0 copy-start
  0.6 10.9 %shard_map.68 = bf16[8,64,512]{2,1,0:T(8,128)(2,1)} custom-call(s32[8,64]{1,0:T(8,128)} %bitcast.5, bf16[384,4096]{1,0:T(8,128)(2,1)} %inv_ref.1, bf16[384,4096]{1,0:T(8,128)(2,1)} %prb_ref.1, bf16[64,32768]{1,0:T(8,128)(2,1)} %cpl_ref.1), custom_call_target="tpu_custom_call" | custom-call | tf_op jit(solution)/shard_map/pallas_call | solution.py:132
  11.6 14.7 %all_to_all.5.rows_ref = bf16[8,64,512]{2,1,0:T(8,128)(2,1)S(1)} all-to-all(bf16[8,64,512]{2,1,0:T(8,128)(2,1)} %shard_map.68), channel_id=1, replica_groups=mesh['region'=8,'sub'=32] {'region'}, dimensions={0} | all-to-all | bytes 1048576 | tf_op jit(solution)/shard_map/all_to_all | solution.py:235
  26.3 0.0 copy-done
  26.3 0.5 shard_map.69
  26.8 1.6 %collective-permute-start = (f32[40,128]{1,0:T(8,128)S(1)}, f32[40,128]{1,0:T(8,128)S(1)}, u32[]{:S(2)}, u32[]{:S(2)}) collective-permute-start(f32[40,128]{1,0:T(8,128)S(1)} %shard_map.69), channel_id=1, source_target_pairs={{0,8},{1,9},{2,10},{3,11},{4,12},{5,13},{6,14},{7,15},{8,0},{9,1},... | collective-permute-start | bytes 61448 | tf_op jit(solution)/shard_map/ppermute | solution.py:246
  28.4 2.2 %collective-permute-done = f32[40,128]{1,0:T(8,128)S(1)} collective-permute-done((f32[40,128]{1,0:T(8,128)S(1)}, f32[40,128]{1,0:T(8,128)S(1)}, u32[]{:S(2)}, u32[]{:S(2)}) %collective-permute-start) | collective-permute-done | bytes 20512 | tf_op jit(solution)/shard_map/ppermute | solution.py:246
  30.6 3.0 %collective-permute-start.1 = (f32[40,128]{1,0:T(8,128)S(1)}, f32[40,128]{1,0:T(8,128)S(1)}, u32[]{:S(2)}, u32[]{:S(2)}) collective-permute-start(f32[40,128]{1,0:T(8,128)S(1)} %add.12), channel_id=1, source_target_pairs={{0,24},{1,25},{2,26},{3,27},{4,28},{5,29},{6,30},{7,31},{8,16},{9,... | collective-permute-start | bytes 61448 | tf_op jit(solution)/shard_map/ppermute | solution.py:246
  33.6 2.0 %collective-permute-done.1 = f32[40,128]{1,0:T(8,128)S(1)} collective-permute-done((f32[40,128]{1,0:T(8,128)S(1)}, f32[40,128]{1,0:T(8,128)S(1)}, u32[]{:S(2)}, u32[]{:S(2)}) %collective-permute-start.1) | collective-permute-done | bytes 20512 | tf_op jit(solution)/shard_map/ppermute | solution.py:246
  35.6 0.9 %collective-permute-start.2 = (f32[40,128]{1,0:T(8,128)S(1)}, f32[40,128]{1,0:T(8,128)S(1)}, u32[]{:S(2)}, u32[]{:S(2)}) collective-permute-start(f32[40,128]{1,0:T(8,128)S(1)} %add.13), channel_id=1, source_target_pairs={{0,1},{1,0},{2,3},{3,2},{4,5},{5,4},{6,7},{7,6},{8,9},{9,8},{10,11... | collective-permute-start | bytes 61448 | tf_op jit(solution)/shard_map/ppermute | solution.py:246
  36.5 2.8 %collective-permute-done.2 = f32[40,128]{1,0:T(8,128)S(1)} collective-permute-done((f32[40,128]{1,0:T(8,128)S(1)}, f32[40,128]{1,0:T(8,128)S(1)}, u32[]{:S(2)}, u32[]{:S(2)}) %collective-permute-start.2) | collective-permute-done | bytes 20512 | tf_op jit(solution)/shard_map/ppermute | solution.py:246
  39.4 5.4 %collective-permute-start.3 = (f32[40,128]{1,0:T(8,128)S(1)}, f32[40,128]{1,0:T(8,128)S(1)}, u32[]{:S(2)}, u32[]{:S(2)}) collective-permute-start(f32[40,128]{1,0:T(8,128)S(1)} %add.14), channel_id=1, source_target_pairs={{0,6},{1,7},{2,4},{3,5},{4,2},{5,3},{6,0},{7,1},{8,14},{9,15},{10,... | collective-permute-start | bytes 61448 | tf_op jit(solution)/shard_map/ppermute | solution.py:246
  44.8 1.8 %collective-permute-done.3 = f32[40,128]{1,0:T(8,128)S(1)} collective-permute-done((f32[40,128]{1,0:T(8,128)S(1)}, f32[40,128]{1,0:T(8,128)S(1)}, u32[]{:S(2)}, u32[]{:S(2)}) %collective-permute-start.3) | collective-permute-done | bytes 20512 | tf_op jit(solution)/shard_map/ppermute | solution.py:246
  46.5 2.0 %collective-permute-start.4 = (f32[40,128]{1,0:T(8,128)S(1)}, f32[40,128]{1,0:T(8,128)S(1)}, u32[]{:S(2)}, u32[]{:S(2)}) collective-permute-start(f32[40,128]{1,0:T(8,128)S(1)} %add.15.sum_ref), channel_id=1, source_target_pairs={{0,2},{1,3},{2,0},{3,1},{4,6},{5,7},{6,4},{7,5},{8,10},{9,11},{10,... | collective-permute-start | bytes 61448 | tf_op jit(solution)/shard_map/ppermute | solution.py:246
  48.5 2.7 %collective-permute-done.4.more_ref = f32[40,128]{1,0:T(8,128)S(1)} collective-permute-done((f32[40,128]{1,0:T(8,128)S(1)}, f32[40,128]{1,0:T(8,128)S(1)}, u32[]{:S(2)}, u32[]{:S(2)}) %collective-permute-start.4) | collective-permute-done | bytes 20512 | tf_op jit(solution)/shard_map/ppermute | solution.py:246
  51.2 3.6 %shard_map.70 = (f32[64,4096]{1,0:T(8,128)}, f32[1,4096]{1,0:T(1,128)}) custom-call(f32[40,128]{1,0:T(8,128)S(1)} %add.15.sum_ref, f32[40,128]{1,0:T(8,128)S(1)} %collective-permute-done.4.more_ref, bf16[8,64,512]{2,1,0:T(8,128)(2,1)S(1)} %all_to_all.5.rows_ref), custom_call_target="tpu_custom_call" | custom-call | tf_op jit(solution)/shard_map/pallas_call | solution.py:247
  (4 shorter events, 0.0 us)
Async XLA Ops:
  0.6 25.7 %copy-start = (f32[4096]{0:T(1024)S(1)}, f32[4096]{0:T(1024)}, u32[]{:S(2)}) copy-start(f32[4096]{0:T(1024)} %param.9) | copy-start | bytes 49156
  26.8 3.8 %collective-permute-start = (f32[40,128]{1,0:T(8,128)S(1)}, f32[40,128]{1,0:T(8,128)S(1)}, u32[]{:S(2)}, u32[]{:S(2)}) collective-permute-start(f32[40,128]{1,0:T(8,128)S(1)} %shard_map.69), channel_id=1, source_target_pairs={{0,8},{1,9},{2,10},{3,11},{4,12},{5,13},{6,14},{7,15},{8,0},{9,1},... | collective-permute-start | bytes 61448 | tf_op jit(solution)/shard_map/ppermute | solution.py:246
  30.6 5.0 %collective-permute-start.1 = (f32[40,128]{1,0:T(8,128)S(1)}, f32[40,128]{1,0:T(8,128)S(1)}, u32[]{:S(2)}, u32[]{:S(2)}) collective-permute-start(f32[40,128]{1,0:T(8,128)S(1)} %add.12), channel_id=1, source_target_pairs={{0,24},{1,25},{2,26},{3,27},{4,28},{5,29},{6,30},{7,31},{8,16},{9,... | collective-permute-start | bytes 61448 | tf_op jit(solution)/shard_map/ppermute | solution.py:246
  35.6 3.8 %collective-permute-start.2 = (f32[40,128]{1,0:T(8,128)S(1)}, f32[40,128]{1,0:T(8,128)S(1)}, u32[]{:S(2)}, u32[]{:S(2)}) collective-permute-start(f32[40,128]{1,0:T(8,128)S(1)} %add.13), channel_id=1, source_target_pairs={{0,1},{1,0},{2,3},{3,2},{4,5},{5,4},{6,7},{7,6},{8,9},{9,8},{10,11... | collective-permute-start | bytes 61448 | tf_op jit(solution)/shard_map/ppermute | solution.py:246
  39.4 7.2 %collective-permute-start.3 = (f32[40,128]{1,0:T(8,128)S(1)}, f32[40,128]{1,0:T(8,128)S(1)}, u32[]{:S(2)}, u32[]{:S(2)}) collective-permute-start(f32[40,128]{1,0:T(8,128)S(1)} %add.14), channel_id=1, source_target_pairs={{0,6},{1,7},{2,4},{3,5},{4,2},{5,3},{6,0},{7,1},{8,14},{9,15},{10,... | collective-permute-start | bytes 61448 | tf_op jit(solution)/shard_map/ppermute | solution.py:246
  46.5 4.7 %collective-permute-start.4 = (f32[40,128]{1,0:T(8,128)S(1)}, f32[40,128]{1,0:T(8,128)S(1)}, u32[]{:S(2)}, u32[]{:S(2)}) collective-permute-start(f32[40,128]{1,0:T(8,128)S(1)} %add.15.sum_ref), channel_id=1, source_target_pairs={{0,2},{1,3},{2,0},{3,1},{4,6},{5,7},{6,4},{7,5},{8,10},{9,11},{10,... | collective-permute-start | bytes 61448 | tf_op jit(solution)/shard_map/ppermute | solution.py:246

commit v3 on v2

--- a/solution.py
+++ b/solution.py
@@ -29,7 +29,7 @@
 def gathered(stage, base, u):
     return stage[pl.ds(base + u // 8 * 8 * BLOCK + u % 8, BLOCK, stride=8), :]
 
-def pieces_kernel(cols_hbm, inv_ref, prb_ref, cpl_ref, out_ref, cols, inv_v, prb_v, cpl_v, a0, a1, p0, p1, c0, c1, solved, sem, cols_sem):
+def pieces_kernel(cols_hbm, inv_ref, prb_ref, cpl_ref, out_ref, cols, inv_v, prb_v, cpl_v, a0, a1, p0, p1, c0, c1, solved, out_v, sem, cols_sem, out_sem):
     nb, ni = inv_ref.shape[0], cpl_ref.shape[0]
     kb = cpl_ref.shape[1] // ROW
     groups, cgroups = nb // 32, ni // 16
@@ -83,14 +83,16 @@
             rhs = [solved[cols[k, g * 16 + u]] for k in range(kb)]
             two.append(jnp.dot(jnp.concatenate(lhs, axis=1), jnp.concatenate(rhs, axis=0), preferred_element_type=jnp.float32))
         turned = jnp.transpose(jnp.concatenate(two, axis=0).astype(jnp.bfloat16), (1, 0))[:RANK]
-        out_ref[2 * g + up // 4, :, (up % 4) * 128 : (up % 4) * 128 + 128] = turned
+        out_v[2 * g + up // 4, :, (up % 4) * 128 : (up % 4) * 128 + 128] = turned
+
+    def out_copy(g):
+        return pltpu.make_async_copy(out_v.at[pl.ds(2 * g, 2)], out_ref.at[pl.ds(2 * g, 2)], out_sem.at[g])
 
     def wait(g):
         for copy in interior_copies(g):
             copy.wait()
 
     def solve_beside(g, sa, sp, na, np_):
-        wait(g + 1)
         for u in range(16):
             solve(g, sa, sp, u)
             for p in (2 * u, 2 * u + 1):
@@ -101,27 +103,32 @@
         solve_spread(0, a0, p0, p)
 
     def two_groups(t, carry):
+        wait(2 * t + 1)
+        wait(2 * t + 2)
         solve_beside(2 * t, a0, p0, a1, p1)
         solve_beside(2 * t + 1, a1, p1, a0, p0)
         return carry
 
     lax.fori_loop(0, groups // 2 - 1, two_groups, 0)
+    wait(groups - 1)
+    for g in range(cgroups):
+        coupling_copy(g).wait()
+    cols_copy.wait()
     solve_beside(groups - 2, a0, p0, a1, p1)
-    coupling_copy(0).wait()
     for u in range(16):
         solve(groups - 1, a1, p1, u)
         for q in range(8 * u, 8 * u + 8):
             couple_spread(0, c0, q)
-    cols_copy.wait()
     for g in range(cgroups):
         here, there = (c0, c1) if g % 2 == 0 else (c1, c0)
-        if g + 1 < cgroups:
-            coupling_copy(g + 1).wait()
         for up in range(8):
             couple(g, here, up)
             if g + 1 < cgroups:
                 for q in range(16 * up, 16 * up + 16):
                     couple_spread(g + 1, there, q)
+        out_copy(g).start()
+    for g in range(cgroups):
+        out_copy(g).wait()
 
 
 def turned_pieces(block_inverse, probes, coupling, columns, regions):
@@ -133,7 +140,7 @@
         pieces_kernel,
         out_shape=jax.ShapeDtypeStruct((regions, RANK, ni * BLOCK // regions), jnp.bfloat16),
         in_specs=[any_place] * 4,
-        out_specs=pl.BlockSpec(memory_space=pltpu.VMEM),
+        out_specs=any_place,
         scratch_shapes=[
             pltpu.SMEM(columns.shape[::-1], jnp.int32),
             pltpu.VMEM(block_inverse.shape, jnp.bfloat16),
@@ -141,8 +148,10 @@
             pltpu.VMEM(coupling.shape, jnp.bfloat16),
             stage, stage, stage, stage, big, big,
             pltpu.VMEM((nb, BLOCK, 128), jnp.bfloat16),
+            pltpu.VMEM((regions, RANK, ni * BLOCK // regions), jnp.bfloat16),
             pltpu.SemaphoreType.DMA((3, nb // 32)),
             pltpu.SemaphoreType.DMA(()),
+            pltpu.SemaphoreType.DMA((ni // 16,)),
         ],
         compiler_params=pltpu.CompilerParams(vmem_limit_bytes=58 * MIB),
     )(columns.T, block_inverse, probes, coupling)
@@ -154,6 +163,34 @@
     middle = rest.astype(jnp.bfloat16)
     low = (rest - middle.astype(jnp.float32)).astype(jnp.bfloat16)
     return jnp.concatenate([high, middle, low], axis=0)
+
+
+def packed_sums(gram, moment):
+    half = gram.shape[0] // 2
+    row_at = lax.broadcasted_iota(jnp.int32, (half, half), 0)
+    lane_at = lax.broadcasted_iota(jnp.int32, (half, half), 1)
+    first, corner, second = gram[:half, :half], gram[:half, half:], gram[half:, half:]
+    square = jnp.concatenate([jnp.where(lane_at >= row_at, first, second), corner], axis=1)
+    diagonal = jnp.sum(jnp.where(lane_at == row_at, second, 0.0), axis=0, keepdims=True)
+    last = jnp.concatenate([moment, diagonal, jnp.zeros_like(diagonal)], axis=1)
+    last = jnp.broadcast_to(last, (8, 4 * half))
+    return jnp.concatenate([jnp.concatenate([square[: half // 2], square[half // 2 :]], axis=1), last], axis=0)
+
+
+def unpacked_sums(packed):
+    half = packed.shape[1] // 4
+    rank = 2 * half
+    row_at = lax.broadcasted_iota(jnp.int32, (half, half), 0)
+    lane_at = lax.broadcasted_iota(jnp.int32, (half, half), 1)
+    square = jnp.concatenate([packed[: half // 2, :rank], packed[: half // 2, rank:]], axis=0)
+    turned = jnp.transpose(jnp.concatenate([square, square], axis=1), (1, 0))
+    upper, lower = square[:, :half], turned[:half]
+    moment, diagonal = packed[half // 2 : half // 2 + 1, :rank], packed[half // 2 : half // 2 + 1, rank : rank + half]
+    first = jnp.where(lane_at >= row_at, upper, lower)
+    second = jnp.where(lane_at >= row_at, lower, upper)
+    second = jnp.where(lane_at == row_at, diagonal, second)
+    top = jnp.concatenate([first, square[:, half:]], axis=1)
+    return jnp.concatenate([top, jnp.concatenate([turned[half:rank], second], axis=1)], axis=0), moment
 
 
 def gram_kernel(rows_ref, res_ref, out_ref):
@@ -165,11 +202,9 @@
         gram += lax.dot_general(y, y, NT, preferred_element_type=jnp.float32)
         parts = three_parts(res_ref[:, r * run : (r + 1) * run])
         moment += lax.dot_general(parts, y, NT, preferred_element_type=jnp.float32)
-    half = rank // 2
-    out_ref[:half, :] = jnp.concatenate([gram[:half], gram[half:]], axis=1)
-    row = moment[0:1] + moment[1:2] + moment[2:3]
-    row = jnp.concatenate([row, jnp.zeros_like(row)], axis=1)
-    out_ref[half:, :] = jnp.broadcast_to(row, (8, 2 * rank))
+    packed = packed_sums(gram, moment[0:1] + moment[1:2] + moment[2:3])
+    for s in range(out_ref.shape[0]):
+        out_ref[s] = packed
 
 
 def two_parts(x):
@@ -201,13 +236,12 @@
     return jnp.concatenate(done, axis=0)
 
 
-def finish_kernel(total_rows, sum_ref, more_ref, rows_ref, basis_ref, corr_ref, basis_v, sem):
+def finish_kernel(total_rows, sums_ref, rows_ref, basis_ref, corr_ref, basis_v, sem):
     regions, rank, run = rows_ref.shape
-    half = rank // 2
-    total = sum_ref[...] + more_ref[...]
-    packed = total[:half]
-    gram = jnp.concatenate([packed[:, :rank], packed[:, rank:]], axis=0)
-    moment = total[half : half + 1, :rank]
+    total = sums_ref[0]
+    for n in range(1, sums_ref.shape[0]):
+        total = total + sums_ref[n]
+    gram, moment = unpacked_sums(total)
     lower_inverse = inverse_lower(gram)
     coefficients = jnp.sum(lower_inverse * moment, axis=1, keepdims=True)
     weights = two_parts(lower_inverse * math.sqrt(total_rows))
@@ -233,28 +267,25 @@
     in_vmem = pl.BlockSpec(memory_space=pltpu.VMEM)
     pieces = turned_pieces(block_inverse, probes, coupling, columns, regions)
     owned = lax.all_to_all(pieces, "region", split_axis=0, concat_axis=0, tiled=True)
-    total = pl.pallas_call(
+    sums = pl.pallas_call(
         gram_kernel,
-        out_shape=jax.ShapeDtypeStruct((RANK // 2 + 8, 2 * RANK), jnp.float32),
+        out_shape=jax.ShapeDtypeStruct((subs, RANK // 4 + 8, 2 * RANK), jnp.float32),
         in_specs=[in_vmem, in_vmem],
         out_specs=in_vmem,
         compiler_params=pltpu.CompilerParams(vmem_limit_bytes=16 * MIB),
     )(owned, residual.reshape(1, rows_here))
-    more = jnp.zeros_like(total)
-    for n, step in enumerate((8, 24, 1, 6, 2)):
-        total = total + more if n else total
-        more = lax.ppermute(total, "sub", [(i, i ^ step) for i in range(subs)])
+    sums = lax.all_to_all(sums, "sub", split_axis=0, concat_axis=0, tiled=True)
     basis_t, correction = pl.pallas_call(
         functools.partial(finish_kernel, rows_here * subs),
         out_shape=(
             jax.ShapeDtypeStruct((RANK, rows_here), jnp.float32),
             jax.ShapeDtypeStruct((1, rows_here), jnp.float32),
         ),
-        in_specs=[in_vmem, in_vmem, in_vmem],
+        in_specs=[in_vmem, in_vmem],
         out_specs=(pl.BlockSpec(memory_space=pl.ANY), in_vmem),
         scratch_shapes=[pltpu.VMEM((RANK, rows_here), jnp.float32), pltpu.SemaphoreType.DMA((regions,))],
         compiler_params=pltpu.CompilerParams(vmem_limit_bytes=16 * MIB),
-    )(total, more, owned)
+    )(sums, owned)
     return basis_t.T, correction.reshape(rows_here)
 
 

time: 55.9 us -> 55.7 us (level); the launches traced: 54.8 us -> 55.5 us
  blocking collectives: 14.7 us -> 40.5 us
  starting transfers between devices: 13 us -> 0 us
  waiting for transfers between devices: 11.5 us -> 0 us
  Pallas kernels: 15 us -> 14.3 us
    all_to_all x0 -> x1, blocking collectives: none -> 25.8 us  [per_device(): sums = lax.all_to_all(sums, 'sub', split_axis=0, concat_axis=0, tiled=True)]
    ppermute x5 -> x0, starting transfers between devices: 13 us -> none  [per_device(): more = lax.ppermute(total, 'sub', [(i, i ^ step) for i in range(subs)])]
    ppermute x5 -> x0, waiting for transfers between devices: 11.5 us -> none  [per_device(): more = lax.ppermute(total, 'sub', [(i, i ^ step) for i in range(subs)])]
    pallas_call x1, Pallas kernels: 10.9 us -> 9.88 us  [turned_pieces(): pl.pallas_call(pieces_kernel, out_shape=jax.ShapeDtypeStruct((regions, RA...]
  transfers between devices with their start and end apart: 5 -> 0, of which waited for: 5 -> 0; matrix products, arithmetic and copies ran while one was open for 0% -> 0% of each run, Pallas kernels for 0% -> 0%
where the time goes in v3:
time: 55.7 us; the launch traced here: 55.5 us
  blocking collectives  40.5 us (73%)
  Pallas kernels  14.3 us (26%)
  between operations  0.66 us (1%)
    all_to_all x1, blocking collectives, per_device(): sums = lax.all_to_all(sums, 'sub', split_axis=0, concat_axis=0, tiled=True)  25.8 us
    all_to_all x1, blocking collectives, per_device(): lax.all_to_all(pieces, 'region', split_axis=0, concat_axis=0, tiled=True)  14.7 us
    pallas_call x1, Pallas kernels, turned_pieces(): pl.pallas_call(pieces_kernel, out_shape=jax.ShapeDtypeStruct((regions, RA...  9.88 us
    pallas_call x1, Pallas kernels, per_device(): pl.pallas_call(functools.partial(finish_kernel, rows_here * subs), out_sh...  3.88 us

profile of v3, /device:TPU:32, one launch (start us, length us, event | category | flops | bytes accessed | tf_op | source)
XLA Modules:
  0.0 55.5 jit_solution(10850259599864699832)
XLA Ops:
  0.6 0.0 copy-start
  0.6 9.9 %shard_map.68 = bf16[8,64,512]{2,1,0:T(8,128)(2,1)} custom-call(s32[8,64]{1,0:T(8,128)} %bitcast.5, bf16[384,4096]{1,0:T(8,128)(2,1)} %inv_ref.1, bf16[384,4096]{1,0:T(8,128)(2,1)} %prb_ref.1, bf16[64,32768]{1,0:T(8,128)(2,1)} %cpl_ref.1), custom_call_target="tpu_custom_call" | custom-call | tf_op jit(solution)/shard_map/pallas_call | solution.py:139
  10.5 14.7 %all_to_all.10.rows_ref = bf16[8,64,512]{2,1,0:T(8,128)(2,1)S(1)} all-to-all(bf16[8,64,512]{2,1,0:T(8,128)(2,1)} %shard_map.68), channel_id=1, replica_groups=mesh['region'=8,'sub'=32] {'region'}, dimensions={0} | all-to-all | bytes 1048576 | tf_op jit(solution)/shard_map/all_to_all | solution.py:269
  25.2 0.0 copy-done
  25.2 0.6 %shard_map.69 = f32[32,24,128]{2,1,0:T(8,128)S(1)} custom-call(bf16[8,64,512]{2,1,0:T(8,128)(2,1)S(1)} %all_to_all.10.rows_ref, f32[1,4096]{1,0:T(1,128)S(1)} %bitcast.4), custom_call_target="tpu_custom_call" | custom-call | tf_op jit(solution)/shard_map/pallas_call | solution.py:270
  25.8 25.8 %all_to_all.11.sums_ref = f32[32,24,128]{2,1,0:T(8,128)S(1)} all-to-all(f32[32,24,128]{2,1,0:T(8,128)S(1)} %shard_map.69), channel_id=1, replica_groups=mesh['region'=8,'sub'=32] {'sub'}, dimensions={0} | all-to-all | bytes 786432 | tf_op jit(solution)/shard_map/all_to_all | solution.py:277
  51.6 3.9 %shard_map.70 = (f32[64,4096]{1,0:T(8,128)}, f32[1,4096]{1,0:T(1,128)}) custom-call(f32[32,24,128]{2,1,0:T(8,128)S(1)} %all_to_all.11.sums_ref, bf16[8,64,512]{2,1,0:T(8,128)(2,1)S(1)} %all_to_all.10.rows_ref), custom_call_target="tpu_custom_call" | custom-call | tf_op jit(solution)/shard_map/pallas_call | solution.py:278
Async XLA Ops:
  0.6 24.6 %copy-start = (f32[4096]{0:T(1024)S(1)}, f32[4096]{0:T(1024)}, u32[]{:S(2)}) copy-start(f32[4096]{0:T(1024)} %param.9) | copy-start | bytes 49156

commit v4 on v3

--- a/solution.py
+++ b/solution.py
@@ -13,21 +13,25 @@
 ROW = BLOCK * BLOCK
 MIB = 2**20
 STEP = 8
-NT = (((1,), (1,)), ((), ()))
 
 
 def spread(src, r0, c0, r1, c1, dst, base, p):
-    x = src[pl.ds(r0, 16), pl.ds(c0 + 128 * p, 128)]
-    y = src[pl.ds(r1, 16), pl.ds(c1 + 128 * p, 128)]
-    even = jnp.concatenate([x[:, :BLOCK], y[:, :BLOCK]], axis=1).astype(jnp.float32)
-    odd = jnp.concatenate([x[:, BLOCK:], y[:, BLOCK:]], axis=1).astype(jnp.float32)
+    x = src[pl.ds(r0, 16), pl.ds(c0 + 128 * p, 256)]
+    y = src[pl.ds(r1, 16), pl.ds(c1 + 128 * p, 256)]
+    x = [x[:, BLOCK * i : BLOCK * i + BLOCK] for i in range(4)]
+    y = [y[:, BLOCK * i : BLOCK * i + BLOCK] for i in range(4)]
+    even = jnp.concatenate([x[0], y[0], x[2], y[2]], axis=1).astype(jnp.float32)
+    odd = jnp.concatenate([x[1], y[1], x[3], y[3]], axis=1).astype(jnp.float32)
     for h in range(2):
-        at = base + 8 * BLOCK * h + 16 * p
-        dst[pl.ds(at, 8), :] = even[8 * h : 8 * h + 8]
-        dst[pl.ds(at + 8, 8), :] = odd[8 * h : 8 * h + 8]
+        for q in range(2):
+            at = base + 8 * BLOCK * h + 16 * (p + q)
+            dst[pl.ds(at, 8), :] = even[8 * h : 8 * h + 8, 128 * q : 128 * q + 128]
+            dst[pl.ds(at + 8, 8), :] = odd[8 * h : 8 * h + 8, 128 * q : 128 * q + 128]
+
 
 def gathered(stage, base, u):
     return stage[pl.ds(base + u // 8 * 8 * BLOCK + u % 8, BLOCK, stride=8), :]
+
 
 def pieces_kernel(cols_hbm, inv_ref, prb_ref, cpl_ref, out_ref, cols, inv_v, prb_v, cpl_v, a0, a1, p0, p1, c0, c1, solved, out_v, sem, cols_sem, out_sem):
     nb, ni = inv_ref.shape[0], cpl_ref.shape[0]
@@ -77,13 +81,14 @@
         spread(cpl_v, r0, 2 * ROW * kp, r0, 2 * ROW * kp + ROW, sc, 16 * BLOCK * kp, p)
 
     def couple(g, sc, up):
-        two = []
-        for u in (2 * up, 2 * up + 1):
+        parts = []
+        for e in range(2):
+            u = up // 4 * 8 + up % 4 + 4 * e
             lhs = [gathered(sc, 16 * BLOCK * kp, u).astype(jnp.bfloat16) for kp in range(kb // 2)]
-            rhs = [solved[cols[k, g * 16 + u]] for k in range(kb)]
-            two.append(jnp.dot(jnp.concatenate(lhs, axis=1), jnp.concatenate(rhs, axis=0), preferred_element_type=jnp.float32))
-        turned = jnp.transpose(jnp.concatenate(two, axis=0).astype(jnp.bfloat16), (1, 0))[:RANK]
-        out_v[2 * g + up // 4, :, (up % 4) * 128 : (up % 4) * 128 + 128] = turned
+            rhs = [solved[cols[k, g * 16 + u] ^ (16 * e)] for k in range(kb)]
+            parts.append(jnp.dot(jnp.concatenate(lhs, axis=1), jnp.concatenate(rhs, axis=0), preferred_element_type=jnp.float32))
+        both = jnp.where(low, parts[0], parts[1]).astype(jnp.bfloat16)
+        out_v[2 * g + up // 4, up % 4 * BLOCK : up % 4 * BLOCK + BLOCK, :] = both
 
     def out_copy(g):
         return pltpu.make_async_copy(out_v.at[pl.ds(2 * g, 2)], out_ref.at[pl.ds(2 * g, 2)], out_sem.at[g])
@@ -95,11 +100,10 @@
     def solve_beside(g, sa, sp, na, np_):
         for u in range(16):
             solve(g, sa, sp, u)
-            for p in (2 * u, 2 * u + 1):
-                solve_spread(g + 1, na, np_, p)
+            solve_spread(g + 1, na, np_, 2 * u)
 
     wait(0)
-    for p in range(32):
+    for p in range(0, BLOCK // 2, 2):
         solve_spread(0, a0, p0, p)
 
     def two_groups(t, carry):
@@ -117,28 +121,28 @@
     solve_beside(groups - 2, a0, p0, a1, p1)
     for u in range(16):
         solve(groups - 1, a1, p1, u)
-        for q in range(8 * u, 8 * u + 8):
+        for q in range(8 * u, 8 * u + 8, 2):
             couple_spread(0, c0, q)
     for g in range(cgroups):
         here, there = (c0, c1) if g % 2 == 0 else (c1, c0)
         for up in range(8):
             couple(g, here, up)
             if g + 1 < cgroups:
-                for q in range(16 * up, 16 * up + 16):
+                for q in range(16 * up, 16 * up + 16, 2):
                     couple_spread(g + 1, there, q)
         out_copy(g).start()
     for g in range(cgroups):
         out_copy(g).wait()
 
 
-def turned_pieces(block_inverse, probes, coupling, columns, regions):
+def paired_pieces(block_inverse, probes, coupling, columns, regions):
     nb, ni = block_inverse.shape[0], coupling.shape[0]
     any_place = pl.BlockSpec(memory_space=pl.ANY)
     stage = pltpu.VMEM((16 * BLOCK, 128), jnp.float32)
     big = pltpu.VMEM((64 * BLOCK, 128), jnp.float32)
     return pl.pallas_call(
         pieces_kernel,
-        out_shape=jax.ShapeDtypeStruct((regions, RANK, ni * BLOCK // regions), jnp.bfloat16),
+        out_shape=jax.ShapeDtypeStruct((regions, ni * BLOCK // regions // 2, 2 * RANK), jnp.bfloat16),
         in_specs=[any_place] * 4,
         out_specs=any_place,
         scratch_shapes=[
@@ -148,7 +152,7 @@
             pltpu.VMEM(coupling.shape, jnp.bfloat16),
             stage, stage, stage, stage, big, big,
             pltpu.VMEM((nb, BLOCK, 128), jnp.bfloat16),
-            pltpu.VMEM((regions, RANK, ni * BLOCK // regions), jnp.bfloat16),
+            pltpu.VMEM((regions, ni * BLOCK // regions // 2, 2 * RANK), jnp.bfloat16),
             pltpu.SemaphoreType.DMA((3, nb // 32)),
             pltpu.SemaphoreType.DMA(()),
             pltpu.SemaphoreType.DMA((ni // 16,)),
@@ -193,18 +197,25 @@
     return jnp.concatenate([top, jnp.concatenate([turned[half:rank], second], axis=1)], axis=0), moment
 
 
-def gram_kernel(rows_ref, res_ref, out_ref):
-    regions, rank, run = rows_ref.shape
-    gram = jnp.zeros((rank, rank), jnp.float32)
-    moment = jnp.zeros((3, rank), jnp.float32)
+def gram_kernel(pairs_ref, res_ref, sums_ref, turned_ref):
+    regions, half, lanes = pairs_ref.shape
+    rank = lanes // 2
+    gram = jnp.zeros((lanes, lanes), jnp.float32)
+    moment = jnp.zeros((6, lanes), jnp.float32)
     for r in range(regions):
-        y = rows_ref[r]
-        gram += lax.dot_general(y, y, NT, preferred_element_type=jnp.float32)
-        parts = three_parts(res_ref[:, r * run : (r + 1) * run])
-        moment += lax.dot_general(parts, y, NT, preferred_element_type=jnp.float32)
+        pairs = pairs_ref[r]
+        at = 2 * r * half
+        turned = jnp.transpose(pairs, (1, 0))
+        turned_ref[:, at : at + half] = turned[:rank]
+        turned_ref[:, at + half : at + 2 * half] = turned[rank:]
+        gram += jnp.dot(turned, pairs, preferred_element_type=jnp.float32)
+        parts = [three_parts(res_ref[:, at + half * i : at + half * i + half]) for i in range(2)]
+        moment += jnp.dot(jnp.concatenate(parts, axis=0), pairs, preferred_element_type=jnp.float32)
+    gram = gram[:rank, :rank] + gram[rank:, rank:]
+    moment = moment[:3, :rank] + moment[3:, rank:]
     packed = packed_sums(gram, moment[0:1] + moment[1:2] + moment[2:3])
-    for s in range(out_ref.shape[0]):
-        out_ref[s] = packed
+    for s in range(sums_ref.shape[0]):
+        sums_ref[s] = packed
 
 
 def two_parts(x):
@@ -237,7 +248,8 @@
 
 
 def finish_kernel(total_rows, sums_ref, rows_ref, basis_ref, corr_ref, basis_v, sem):
-    regions, rank, run = rows_ref.shape
+    rank, run = rows_ref.shape[0], rows_ref.shape[1] // sem.shape[0]
+    regions = sem.shape[0]
     total = sums_ref[0]
     for n in range(1, sums_ref.shape[0]):
         total = total + sums_ref[n]
@@ -252,7 +264,7 @@
         return pltpu.make_async_copy(basis_v.at[:, cols], basis_ref.at[:, cols], sem.at[r])
 
     for r in range(regions):
-        q = jnp.dot(weights, rows_ref[r], preferred_element_type=jnp.float32)
+        q = jnp.dot(weights, rows_ref[:, r * run : (r + 1) * run], preferred_element_type=jnp.float32)
         q = q[:rank] + q[rank:]
         basis_v[:, r * run : (r + 1) * run] = q
         copy_out(r).start()
@@ -265,13 +277,16 @@
     regions, subs = lax.axis_size("region"), lax.axis_size("sub")
     rows_here = residual.shape[0]
     in_vmem = pl.BlockSpec(memory_space=pltpu.VMEM)
-    pieces = turned_pieces(block_inverse, probes, coupling, columns, regions)
+    pieces = paired_pieces(block_inverse, probes, coupling, columns, regions)
     owned = lax.all_to_all(pieces, "region", split_axis=0, concat_axis=0, tiled=True)
-    sums = pl.pallas_call(
+    sums, turned = pl.pallas_call(
         gram_kernel,
-        out_shape=jax.ShapeDtypeStruct((subs, RANK // 4 + 8, 2 * RANK), jnp.float32),
+        out_shape=(
+            jax.ShapeDtypeStruct((subs, RANK // 4 + 8, 2 * RANK), jnp.float32),
+            jax.ShapeDtypeStruct((RANK, rows_here), jnp.bfloat16),
+        ),
         in_specs=[in_vmem, in_vmem],
-        out_specs=in_vmem,
+        out_specs=(in_vmem, in_vmem),
         compiler_params=pltpu.CompilerParams(vmem_limit_bytes=16 * MIB),
     )(owned, residual.reshape(1, rows_here))
     sums = lax.all_to_all(sums, "sub", split_axis=0, concat_axis=0, tiled=True)
@@ -285,7 +300,7 @@
         out_specs=(pl.BlockSpec(memory_space=pl.ANY), in_vmem),
         scratch_shapes=[pltpu.VMEM((RANK, rows_here), jnp.float32), pltpu.SemaphoreType.DMA((regions,))],
         compiler_params=pltpu.CompilerParams(vmem_limit_bytes=16 * MIB),
-    )(sums, owned)
+    )(sums, turned)
     return basis_t.T, correction.reshape(rows_here)
 
 

time: 55.7 us -> 54.7 us (0.982)
  Pallas kernels: 14.3 us -> 13.3 us
    pallas_call x2, Pallas kernels: 10.4 us -> 9.46 us  [the longest x1 8.81 us: paired_pieces(): pl.pallas_call(pieces_kernel, out_shape=jax.ShapeDtypeStruct((regions, ni...]
where the time goes in v4:
time: 54.7 us; the launch traced here: 54.5 us
  blocking collectives  40.5 us (74%)
  Pallas kernels  13.3 us (24%)
  between operations  0.66 us (1%)
    all_to_all x1, blocking collectives, per_device(): sums = lax.all_to_all(sums, 'sub', split_axis=0, concat_axis=0, tiled=True)  25.8 us
    all_to_all x1, blocking collectives, per_device(): lax.all_to_all(pieces, 'region', split_axis=0, concat_axis=0, tiled=True)  14.7 us
    pallas_call x1, Pallas kernels, paired_pieces(): pl.pallas_call(pieces_kernel, out_shape=jax.ShapeDtypeStruct((regions, ni...  8.81 us
    pallas_call x1, Pallas kernels, per_device(): pl.pallas_call(functools.partial(finish_kernel, rows_here * subs), out_sh...  3.87 us

profile of v4, /device:TPU:32, one launch (start us, length us, event | category | flops | bytes accessed | tf_op | source)
XLA Modules:
  0.0 54.5 jit_solution(1836065936538279369)
XLA Ops:
  0.6 0.0 copy-start
  0.6 8.8 %shard_map.68 = bf16[8,256,128]{2,1,0:T(8,128)(2,1)} custom-call(s32[8,64]{1,0:T(8,128)} %bitcast.5, bf16[384,4096]{1,0:T(8,128)(2,1)} %inv_ref.1, bf16[384,4096]{1,0:T(8,128)(2,1)} %prb_ref.1, bf16[64,32768]{1,0:T(8,128)(2,1)} %cpl_ref.1), custom_call_target="tpu_custom_call" | custom-call | tf_op jit(solution)/shard_map/pallas_call | solution.py:143
  9.5 14.7 %all_to_all.10.pairs_ref = bf16[8,256,128]{2,1,0:T(8,128)(2,1)S(1)} all-to-all(bf16[8,256,128]{2,1,0:T(8,128)(2,1)} %shard_map.68), channel_id=1, replica_groups=mesh['region'=8,'sub'=32] {'region'}, dimensions={0} | all-to-all | bytes 1048576 | tf_op jit(solution)/shard_map/all_to_all | solution.py:281
  24.2 0.0 copy-done
  24.2 0.7 %shard_map.69 = (f32[32,24,128]{2,1,0:T(8,128)S(1)}, bf16[64,4096]{1,0:T(8,128)(2,1)S(1)}) custom-call(bf16[8,256,128]{2,1,0:T(8,128)(2,1)S(1)} %all_to_all.10.pairs_ref, f32[1,4096]{1,0:T(1,128)S(1)} %bitcast.4), custom_call_target="tpu_custom_call" | custom-call | tf_op jit(solution)/shard_map/pallas_call | solution.py:282
  24.8 25.8 %all_to_all.11.sums_ref = f32[32,24,128]{2,1,0:T(8,128)S(1)} all-to-all(f32[32,24,128]{2,1,0:T(8,128)S(1)} %get-tuple-element.6), channel_id=1, replica_groups=mesh['region'=8,'sub'=32] {'sub'}, dimensions={0} | all-to-all | bytes 786432 | tf_op jit(solution)/shard_map/all_to_all | solution.py:292
  50.6 3.9 %shard_map.70 = (f32[64,4096]{1,0:T(8,128)}, f32[1,4096]{1,0:T(1,128)}) custom-call(f32[32,24,128]{2,1,0:T(8,128)S(1)} %all_to_all.11.sums_ref, bf16[64,4096]{1,0:T(8,128)(2,1)S(1)} %get-tuple-element.7.rows_ref), custom_call_target="tpu_custom_call" | custom-call | tf_op jit(solution)/shard_map/pallas_call | solution.py:293
Async XLA Ops:
  0.6 23.5 %copy-start = (f32[4096]{0:T(1024)S(1)}, f32[4096]{0:T(1024)}, u32[]{:S(2)}) copy-start(f32[4096]{0:T(1024)} %param.9) | copy-start | bytes 49156

commit v5 on v4

--- a/solution.py
+++ b/solution.py
@@ -12,7 +12,7 @@
 RANK = 64
 ROW = BLOCK * BLOCK
 MIB = 2**20
-STEP = 8
+STEP = 16
 
 
 def spread(src, r0, c0, r1, c1, dst, base, p):
@@ -177,12 +177,14 @@
     square = jnp.concatenate([jnp.where(lane_at >= row_at, first, second), corner], axis=1)
     diagonal = jnp.sum(jnp.where(lane_at == row_at, second, 0.0), axis=0, keepdims=True)
     last = jnp.concatenate([moment, diagonal, jnp.zeros_like(diagonal)], axis=1)
-    last = jnp.broadcast_to(last, (8, 4 * half))
-    return jnp.concatenate([jnp.concatenate([square[: half // 2], square[half // 2 :]], axis=1), last], axis=0)
+    square = jnp.concatenate([square[: half // 2], square[half // 2 :]], axis=1)
+    return [square[i : i + 1] for i in range(half // 2)] + [last]
 
 
 def unpacked_sums(packed):
-    half = packed.shape[1] // 4
+    lanes = 2 * RANK
+    packed = jnp.concatenate([packed[:, i : i + lanes] for i in range(0, packed.shape[1], lanes)], axis=0)
+    half = lanes // 4
     rank = 2 * half
     row_at = lax.broadcasted_iota(jnp.int32, (half, half), 0)
     lane_at = lax.broadcasted_iota(jnp.int32, (half, half), 1)
@@ -214,8 +216,9 @@
     gram = gram[:rank, :rank] + gram[rank:, rank:]
     moment = moment[:3, :rank] + moment[3:, rank:]
     packed = packed_sums(gram, moment[0:1] + moment[1:2] + moment[2:3])
-    for s in range(sums_ref.shape[0]):
-        sums_ref[s] = packed
+    for i, row in enumerate(packed):
+        for s in range(sums_ref.shape[0]):
+            sums_ref[s, :, lanes * i : lanes * i + lanes] = row
 
 
 def two_parts(x):
@@ -282,7 +285,7 @@
     sums, turned = pl.pallas_call(
         gram_kernel,
         out_shape=(
-            jax.ShapeDtypeStruct((subs, RANK // 4 + 8, 2 * RANK), jnp.float32),
+            jax.ShapeDtypeStruct((subs, 1, (RANK // 4 + 1) * 2 * RANK), jnp.float32),
             jax.ShapeDtypeStruct((RANK, rows_here), jnp.bfloat16),
         ),
         in_specs=[in_vmem, in_vmem],

time: 54.7 us -> 52.3 us (0.956)
  blocking collectives: 40.5 us -> 38.1 us
    all_to_all x1, blocking collectives: 25.8 us -> 23.4 us  [per_device(): sums = lax.all_to_all(sums, 'sub', split_axis=0, concat_axis=0, tiled=True)]
where the time goes in v5:
time: 52.3 us; the launch traced here: 52.1 us
  blocking collectives  38.1 us (73%)
  Pallas kernels  13.3 us (25%)
  between operations  0.66 us (1%)
    all_to_all x1, blocking collectives, per_device(): sums = lax.all_to_all(sums, 'sub', split_axis=0, concat_axis=0, tiled=True)  23.4 us
    all_to_all x1, blocking collectives, per_device(): lax.all_to_all(pieces, 'region', split_axis=0, concat_axis=0, tiled=True)  14.7 us
    pallas_call x1, Pallas kernels, paired_pieces(): pl.pallas_call(pieces_kernel, out_shape=jax.ShapeDtypeStruct((regions, ni...  8.81 us
    pallas_call x1, Pallas kernels, per_device(): pl.pallas_call(functools.partial(finish_kernel, rows_here * subs), out_sh...  3.74 us

profile of v5, /device:TPU:32, one launch (start us, length us, event | category | flops | bytes accessed | tf_op | source)
XLA Modules:
  0.0 52.1 jit_solution(1725232884478071893)
XLA Ops:
  0.6 0.0 copy-start
  0.6 8.8 %shard_map.68 = bf16[8,256,128]{2,1,0:T(8,128)(2,1)} custom-call(s32[8,64]{1,0:T(8,128)} %bitcast.5, bf16[384,4096]{1,0:T(8,128)(2,1)} %inv_ref.1, bf16[384,4096]{1,0:T(8,128)(2,1)} %prb_ref.1, bf16[64,32768]{1,0:T(8,128)(2,1)} %cpl_ref.1), custom_call_target="tpu_custom_call" | custom-call | tf_op jit(solution)/shard_map/pallas_call | solution.py:143
  9.5 14.7 %all_to_all.10.pairs_ref = bf16[8,256,128]{2,1,0:T(8,128)(2,1)S(1)} all-to-all(bf16[8,256,128]{2,1,0:T(8,128)(2,1)} %shard_map.68), channel_id=1, replica_groups=mesh['region'=8,'sub'=32] {'region'}, dimensions={0} | all-to-all | bytes 1048576 | tf_op jit(solution)/shard_map/all_to_all | solution.py:284
  24.2 0.0 copy-done
  24.2 0.8 %shard_map.69 = (f32[32,1,2176]{2,1,0:T(1,128)S(1)}, bf16[64,4096]{1,0:T(8,128)(2,1)S(1)}) custom-call(bf16[8,256,128]{2,1,0:T(8,128)(2,1)S(1)} %all_to_all.10.pairs_ref, f32[1,4096]{1,0:T(1,128)S(1)} %bitcast.4), custom_call_target="tpu_custom_call" | custom-call | tf_op jit(solution)/shard_map/pallas_call | solution.py:285
  24.9 23.4 %all_to_all.11.sums_ref = f32[32,1,2176]{2,1,0:T(1,128)S(1)} all-to-all(f32[32,1,2176]{2,1,0:T(1,128)S(1)} %get-tuple-element.6), channel_id=1, replica_groups=mesh['region'=8,'sub'=32] {'sub'}, dimensions={0} | all-to-all | bytes 557056 | tf_op jit(solution)/shard_map/all_to_all | solution.py:295
  48.4 3.7 %shard_map.70 = (f32[64,4096]{1,0:T(8,128)}, f32[1,4096]{1,0:T(1,128)}) custom-call(f32[32,1,2176]{2,1,0:T(1,128)S(1)} %all_to_all.11.sums_ref, bf16[64,4096]{1,0:T(8,128)(2,1)S(1)} %get-tuple-element.7.rows_ref), custom_call_target="tpu_custom_call" | custom-call | tf_op jit(solution)/shard_map/pallas_call | solution.py:296
Async XLA Ops:
  0.6 23.5 %copy-start = (f32[4096]{0:T(1024)S(1)}, f32[4096]{0:T(1024)}, u32[]{:S(2)}) copy-start(f32[4096]{0:T(1024)} %param.9) | copy-start | bytes 49156

commit v6 on v5

--- a/solution.py
+++ b/solution.py
@@ -13,6 +13,7 @@
 ROW = BLOCK * BLOCK
 MIB = 2**20
 STEP = 16
+SUB_Y = 4
 
 
 def spread(src, r0, c0, r1, c1, dst, base, p):
@@ -217,8 +218,7 @@
     moment = moment[:3, :rank] + moment[3:, rank:]
     packed = packed_sums(gram, moment[0:1] + moment[1:2] + moment[2:3])
     for i, row in enumerate(packed):
-        for s in range(sums_ref.shape[0]):
-            sums_ref[s, :, lanes * i : lanes * i + lanes] = row
+        sums_ref[0, :, lanes * i : lanes * i + lanes] = row
 
 
 def two_parts(x):
@@ -285,14 +285,19 @@
     sums, turned = pl.pallas_call(
         gram_kernel,
         out_shape=(
-            jax.ShapeDtypeStruct((subs, 1, (RANK // 4 + 1) * 2 * RANK), jnp.float32),
+            jax.ShapeDtypeStruct((1, 1, (RANK // 4 + 1) * 2 * RANK), jnp.float32),
             jax.ShapeDtypeStruct((RANK, rows_here), jnp.bfloat16),
         ),
         in_specs=[in_vmem, in_vmem],
         out_specs=(in_vmem, in_vmem),
         compiler_params=pltpu.CompilerParams(vmem_limit_bytes=16 * MIB),
     )(owned, residual.reshape(1, rows_here))
-    sums = lax.all_to_all(sums, "sub", split_axis=0, concat_axis=0, tiled=True)
+    near = subs // SUB_Y
+    sums = sums + lax.ppermute(sums, "sub", [(i, i ^ near) for i in range(subs)])
+    outer = [i for i in range(subs) if i // near % 4 in (0, 3)]
+    inner = [i for i in range(subs) if i // near % 4 in (1, 2)]
+    sums = jnp.broadcast_to(sums, (subs // 2,) + sums.shape[1:])
+    sums = lax.all_to_all(sums, "sub", split_axis=0, concat_axis=0, tiled=True, axis_index_groups=[outer, inner])
     basis_t, correction = pl.pallas_call(
         functools.partial(finish_kernel, rows_here * subs),
         out_shape=(

time: 52.3 us -> 52.6 us (level)
  blocking collectives: 38.1 us -> 34.7 us
  waiting for transfers between devices: 0 us -> 2.08 us
  starting transfers between devices: 0 us -> 1.65 us
    all_to_all x1, blocking collectives: 23.4 us -> 20 us  [per_device(): lax.all_to_all(sums, 'sub', split_axis=0, concat_axis=0, tiled=True, axis...]
    ppermute x0 -> x1, waiting for transfers between devices: none -> 2.08 us  [per_device(): lax.ppermute(sums, 'sub', [(i, i ^ near) for i in range(subs)])]
    ppermute x0 -> x1, starting transfers between devices: none -> 1.65 us  [per_device(): lax.ppermute(sums, 'sub', [(i, i ^ near) for i in range(subs)])]
  transfers between devices with their start and end apart: 0 -> 1, of which waited for: 0 -> 1; matrix products, arithmetic and copies ran while one was open for 0% -> 0% of each run, Pallas kernels for 0% -> 0%
where the time goes in v6:
time: 52.6 us; the launch traced here: 52.4 us
  blocking collectives  34.7 us (66%)
  Pallas kernels  13.2 us (25%)
  waiting for transfers between devices  2.08 us (4%)
  starting transfers between devices  1.65 us (3%)
  between operations  0.66 us (1%)
    all_to_all x1, blocking collectives, per_device(): lax.all_to_all(sums, 'sub', split_axis=0, concat_axis=0, tiled=True, axis...  20 us
    all_to_all x1, blocking collectives, per_device(): lax.all_to_all(pieces, 'region', split_axis=0, concat_axis=0, tiled=True)  14.7 us
    pallas_call x1, Pallas kernels, paired_pieces(): pl.pallas_call(pieces_kernel, out_shape=jax.ShapeDtypeStruct((regions, ni...  8.81 us
    pallas_call x1, Pallas kernels, per_device(): pl.pallas_call(functools.partial(finish_kernel, rows_here * subs), out_sh...  3.72 us
    ppermute x1, waiting for transfers between devices, per_device(): lax.ppermute(sums, 'sub', [(i, i ^ near) for i in range(subs)])  2.08 us
    ppermute x1, starting transfers between devices, per_device(): lax.ppermute(sums, 'sub', [(i, i ^ near) for i in range(subs)])  1.65 us
  transfers between devices with their start and end apart: 1, of which 1 were waited for; matrix products, arithmetic and copies ran while one was open for 0% of the time, Pallas kernels for 0%

profile of v6, /device:TPU:32, one launch (start us, length us, event | category | flops | bytes accessed | tf_op | source)
XLA Modules:
  0.0 52.4 jit_solution(9104440823605136538)
XLA Ops:
  0.6 0.0 copy-start
  0.6 8.8 %shard_map.68 = bf16[8,256,128]{2,1,0:T(8,128)(2,1)} custom-call(s32[8,64]{1,0:T(8,128)} %bitcast.5, bf16[384,4096]{1,0:T(8,128)(2,1)} %inv_ref.1, bf16[384,4096]{1,0:T(8,128)(2,1)} %prb_ref.1, bf16[64,32768]{1,0:T(8,128)(2,1)} %cpl_ref.1), custom_call_target="tpu_custom_call" | custom-call | tf_op jit(solution)/shard_map/pallas_call | solution.py:144
  9.5 14.7 %all_to_all.10.pairs_ref = bf16[8,256,128]{2,1,0:T(8,128)(2,1)S(1)} all-to-all(bf16[8,256,128]{2,1,0:T(8,128)(2,1)} %shard_map.68), channel_id=1, replica_groups=mesh['region'=8,'sub'=32] {'region'}, dimensions={0} | all-to-all | bytes 1048576 | tf_op jit(solution)/shard_map/all_to_all | solution.py:284
  24.2 0.0 copy-done
  24.2 0.6 %shard_map.69 = (f32[1,1,2176]{2,1,0:T(1,128)S(1)}, bf16[64,4096]{1,0:T(8,128)(2,1)S(1)}) custom-call(bf16[8,256,128]{2,1,0:T(8,128)(2,1)S(1)} %all_to_all.10.pairs_ref, f32[1,4096]{1,0:T(1,128)S(1)} %bitcast.4), custom_call_target="tpu_custom_call" | custom-call | tf_op jit(solution)/shard_map/pallas_call | solution.py:285
  24.8 1.6 %collective-permute-start = (f32[1,1,2176]{2,1,0:T(1,128)S(1)}, f32[1,1,2176]{2,1,0:T(1,128)S(1)}, u32[]{:S(2)}, u32[]{:S(2)}) collective-permute-start(f32[1,1,2176]{2,1,0:T(1,128)S(1)} %get-tuple-element.6), channel_id=1, source_target_pairs={{0,8},{1,9},{2,10},{3,11},{4,12},{5,13},{6,14},{7,15},{8,0},{9,1},... | collective-permute-start | bytes 26120 | tf_op jit(solution)/shard_map/ppermute | solution.py:296
  26.5 2.1 %collective-permute-done = f32[1,1,2176]{2,1,0:T(1,128)S(1)} collective-permute-done((f32[1,1,2176]{2,1,0:T(1,128)S(1)}, f32[1,1,2176]{2,1,0:T(1,128)S(1)}, u32[]{:S(2)}, u32[]{:S(2)}) %collective-permute-start) | collective-permute-done | bytes 8736 | tf_op jit(solution)/shard_map/ppermute | solution.py:296
  28.6 0.1 broadcast_in_dim.8
  28.7 20.0 %all_to_all.11.sums_ref = f32[16,1,2176]{2,1,0:T(1,128)S(1)} all-to-all(f32[16,1,2176]{2,1,0:T(1,128)S(1)} %broadcast_in_dim.8), channel_id=1, replica_groups={{0,1,2,3,4,5,6,7,24,25,26,27,28,29,30,31},{8,9,10,11,12,13,14,15,16,17,..., dimensions={0} | all-to-all | bytes 278528 | tf_op jit(solution)/shard_map/all_to_all | solution.py:300
  48.7 3.7 %shard_map.70 = (f32[64,4096]{1,0:T(8,128)}, f32[1,4096]{1,0:T(1,128)}) custom-call(f32[16,1,2176]{2,1,0:T(1,128)S(1)} %all_to_all.11.sums_ref, bf16[64,4096]{1,0:T(8,128)(2,1)S(1)} %get-tuple-element.7.rows_ref), custom_call_target="tpu_custom_call" | custom-call | tf_op jit(solution)/shard_map/pallas_call | solution.py:301
  (1 shorter events, 0.0 us)
Async XLA Ops:
  0.6 23.5 %copy-start = (f32[4096]{0:T(1024)S(1)}, f32[4096]{0:T(1024)}, u32[]{:S(2)}) copy-start(f32[4096]{0:T(1024)} %param.9) | copy-start | bytes 49156
  24.8 3.7 %collective-permute-start = (f32[1,1,2176]{2,1,0:T(1,128)S(1)}, f32[1,1,2176]{2,1,0:T(1,128)S(1)}, u32[]{:S(2)}, u32[]{:S(2)}) collective-permute-start(f32[1,1,2176]{2,1,0:T(1,128)S(1)} %get-tuple-element.6), channel_id=1, source_target_pairs={{0,8},{1,9},{2,10},{3,11},{4,12},{5,13},{6,14},{7,15},{8,0},{9,1},... | collective-permute-start | bytes 26120 | tf_op jit(solution)/shard_map/ppermute | solution.py:296

commit v7 on v6

--- a/solution.py
+++ b/solution.py
@@ -293,11 +293,11 @@
         compiler_params=pltpu.CompilerParams(vmem_limit_bytes=16 * MIB),
     )(owned, residual.reshape(1, rows_here))
     near = subs // SUB_Y
-    sums = sums + lax.ppermute(sums, "sub", [(i, i ^ near) for i in range(subs)])
-    outer = [i for i in range(subs) if i // near % 4 in (0, 3)]
-    inner = [i for i in range(subs) if i // near % 4 in (1, 2)]
-    sums = jnp.broadcast_to(sums, (subs // 2,) + sums.shape[1:])
-    sums = lax.all_to_all(sums, "sub", split_axis=0, concat_axis=0, tiled=True, axis_index_groups=[outer, inner])
+    for step in (near, 3 * near):
+        sums = sums + lax.ppermute(sums, "sub", [(i, i ^ step) for i in range(subs)])
+    columns_z = [[near * y + z for z in range(near)] for y in range(SUB_Y)]
+    sums = jnp.broadcast_to(sums, (near,) + sums.shape[1:])
+    sums = lax.all_to_all(sums, "sub", split_axis=0, concat_axis=0, tiled=True, axis_index_groups=columns_z)
     basis_t, correction = pl.pallas_call(
         functools.partial(finish_kernel, rows_here * subs),
         out_shape=(

time: 52.6 us -> 54.2 us (1.030)
  the two profiles are of different devices: /device:TPU:32 before, /device:TPU:24 now
where the time goes in v7:
time: 54.2 us; the launch traced here: 54 us
  blocking collectives  31.4 us (58%)
  Pallas kernels  13.2 us (24%)
  waiting for transfers between devices  6.72 us (12%)
  starting transfers between devices  1.96 us (4%)
  between operations  0.67 us (1%)
    all_to_all x1, blocking collectives, per_device(): lax.all_to_all(sums, 'sub', split_axis=0, concat_axis=0, tiled=True, axis...  16.7 us
    all_to_all x1, blocking collectives, per_device(): lax.all_to_all(pieces, 'region', split_axis=0, concat_axis=0, tiled=True)  14.7 us
    pallas_call x1, Pallas kernels, paired_pieces(): pl.pallas_call(pieces_kernel, out_shape=jax.ShapeDtypeStruct((regions, ni...  8.81 us
    ppermute x2, waiting for transfers between devices, per_device(): lax.ppermute(sums, 'sub', [(i, i ^ step) for i in range(subs)])  6.72 us
    pallas_call x1, Pallas kernels, per_device(): pl.pallas_call(functools.partial(finish_kernel, rows_here * subs), out_sh...  3.71 us
    ppermute x2, starting transfers between devices, per_device(): lax.ppermute(sums, 'sub', [(i, i ^ step) for i in range(subs)])  1.96 us
  transfers between devices with their start and end apart: 2, of which 2 were waited for; matrix products, arithmetic and copies ran while one was open for 0% of the time, Pallas kernels for 0%

profile of v7, /device:TPU:24, one launch (start us, length us, event | category | flops | bytes accessed | tf_op | source)
XLA Modules:
  0.0 54.0 jit_solution(1358507012464332120)
XLA Ops:
  0.6 0.0 copy-start
  0.6 8.8 %shard_map.68 = bf16[8,256,128]{2,1,0:T(8,128)(2,1)} custom-call(s32[8,64]{1,0:T(8,128)} %bitcast.5, bf16[384,4096]{1,0:T(8,128)(2,1)} %inv_ref.1, bf16[384,4096]{1,0:T(8,128)(2,1)} %prb_ref.1, bf16[64,32768]{1,0:T(8,128)(2,1)} %cpl_ref.1), custom_call_target="tpu_custom_call" | custom-call | tf_op jit(solution)/shard_map/pallas_call | solution.py:144
  9.5 14.7 %all_to_all.10.pairs_ref = bf16[8,256,128]{2,1,0:T(8,128)(2,1)S(1)} all-to-all(bf16[8,256,128]{2,1,0:T(8,128)(2,1)} %shard_map.68), channel_id=1, replica_groups=mesh['region'=8,'sub'=32] {'region'}, dimensions={0} | all-to-all | bytes 1048576 | tf_op jit(solution)/shard_map/all_to_all | solution.py:284
  24.2 0.0 copy-done
  24.2 0.6 %shard_map.69 = (f32[1,1,2176]{2,1,0:T(1,128)S(1)}, bf16[64,4096]{1,0:T(8,128)(2,1)S(1)}) custom-call(bf16[8,256,128]{2,1,0:T(8,128)(2,1)S(1)} %all_to_all.10.pairs_ref, f32[1,4096]{1,0:T(1,128)S(1)} %bitcast.4), custom_call_target="tpu_custom_call" | custom-call | tf_op jit(solution)/shard_map/pallas_call | solution.py:285
  24.8 0.8 %collective-permute-start = (f32[1,1,2176]{2,1,0:T(1,128)S(1)}, f32[1,1,2176]{2,1,0:T(1,128)S(1)}, u32[]{:S(2)}, u32[]{:S(2)}) collective-permute-start(f32[1,1,2176]{2,1,0:T(1,128)S(1)} %get-tuple-element.6), channel_id=1, source_target_pairs={{0,8},{1,9},{2,10},{3,11},{4,12},{5,13},{6,14},{7,15},{8,0},{9,1},... | collective-permute-start | bytes 26120 | tf_op jit(solution)/shard_map/ppermute | solution.py:297
  25.6 2.9 %collective-permute-done = f32[1,1,2176]{2,1,0:T(1,128)S(1)} collective-permute-done((f32[1,1,2176]{2,1,0:T(1,128)S(1)}, f32[1,1,2176]{2,1,0:T(1,128)S(1)}, u32[]{:S(2)}, u32[]{:S(2)}) %collective-permute-start) | collective-permute-done | bytes 8736 | tf_op jit(solution)/shard_map/ppermute | solution.py:297
  28.6 1.1 %collective-permute-start.1 = (f32[1,1,2176]{2,1,0:T(1,128)S(1)}, f32[1,1,2176]{2,1,0:T(1,128)S(1)}, u32[]{:S(2)}, u32[]{:S(2)}) collective-permute-start(f32[1,1,2176]{2,1,0:T(1,128)S(1)} %add.6), channel_id=1, source_target_pairs={{0,24},{1,25},{2,26},{3,27},{4,28},{5,29},{6,30},{7,31},{8,16},{9,... | collective-permute-start | bytes 26120 | tf_op jit(solution)/shard_map/ppermute | solution.py:297
  29.7 3.8 %collective-permute-done.1 = f32[1,1,2176]{2,1,0:T(1,128)S(1)} collective-permute-done((f32[1,1,2176]{2,1,0:T(1,128)S(1)}, f32[1,1,2176]{2,1,0:T(1,128)S(1)}, u32[]{:S(2)}, u32[]{:S(2)}) %collective-permute-start.1) | collective-permute-done | bytes 8736 | tf_op jit(solution)/shard_map/ppermute | solution.py:297
  33.6 16.7 %all_to_all.11.sums_ref = f32[8,1,2176]{2,1,0:T(1,128)S(1)} all-to-all(f32[8,1,2176]{2,1,0:T(1,128)S(1)} %broadcast_in_dim.8), channel_id=1, replica_groups={{0,1,2,3,4,5,6,7},{8,9,10,11,12,13,14,15},{16,17,18,19,20,21,22,23},{24..., dimensions={0} | all-to-all | bytes 139264 | tf_op jit(solution)/shard_map/all_to_all | solution.py:300
  50.3 3.7 %shard_map.70 = (f32[64,4096]{1,0:T(8,128)}, f32[1,4096]{1,0:T(1,128)}) custom-call(f32[8,1,2176]{2,1,0:T(1,128)S(1)} %all_to_all.11.sums_ref, bf16[64,4096]{1,0:T(8,128)(2,1)S(1)} %get-tuple-element.7.rows_ref), custom_call_target="tpu_custom_call" | custom-call | tf_op jit(solution)/shard_map/pallas_call | solution.py:301
  (3 shorter events, 0.1 us)
Async XLA Ops:
  0.6 23.5 %copy-start = (f32[4096]{0:T(1024)S(1)}, f32[4096]{0:T(1024)}, u32[]{:S(2)}) copy-start(f32[4096]{0:T(1024)} %param.9) | copy-start | bytes 49156
  24.8 3.7 %collective-permute-start = (f32[1,1,2176]{2,1,0:T(1,128)S(1)}, f32[1,1,2176]{2,1,0:T(1,128)S(1)}, u32[]{:S(2)}, u32[]{:S(2)}) collective-permute-start(f32[1,1,2176]{2,1,0:T(1,128)S(1)} %get-tuple-element.6), channel_id=1, source_target_pairs={{0,8},{1,9},{2,10},{3,11},{4,12},{5,13},{6,14},{7,15},{8,0},{9,1},... | collective-permute-start | bytes 26120 | tf_op jit(solution)/shard_map/ppermute | solution.py:297
  28.6 5.0 %collective-permute-start.1 = (f32[1,1,2176]{2,1,0:T(1,128)S(1)}, f32[1,1,2176]{2,1,0:T(1,128)S(1)}, u32[]{:S(2)}, u32[]{:S(2)}) collective-permute-start(f32[1,1,2176]{2,1,0:T(1,128)S(1)} %add.6), channel_id=1, source_target_pairs={{0,24},{1,25},{2,26},{3,27},{4,28},{5,29},{6,30},{7,31},{8,16},{9,... | collective-permute-start | bytes 26120 | tf_op jit(solution)/shard_map/ppermute | solution.py:297
